TPU v7x, 128 devices: a whole 4x4x4 slice. The times are simulated.
128 devices in a mesh: dp: 8 (over y_lo, z), tensor: 16 (over x, y_hi, core).
Axes of the slice: x: 4, y: 4 (y_hi: 2, y_lo: 2; y = y_hi * 2 + y_lo), z: 4, core: 2. Of those that a mesh axis runs over, the one named last changes fastest.
Arguments:
- acts: bfloat16 [8192, 8192], P('dp', 'tensor'), may hold values from -1.265625 to 1.265625, as said below
- grad_out: bfloat16 [8192, 6144], P(('dp', 'tensor')), may hold values from -6 to 6
- weight: bfloat16 [8192, 6144], P('tensor'), may hold values from -0.078125 to 0.078125
- residue: bfloat16 [8, 8192, 6144], P('dp', 'tensor'), may hold values from -40 to 40, as said below
- start_q: float32 [6144, 32], replicated, may hold values from -6 to 6
Outputs:
- grad_in: bfloat16 [8192, 8192], P('dp', 'tensor')
- p_factor: float32 [8192, 32], P('tensor')
- q_factor: float32 [6144, 32], replicated
- new_residue: bfloat16 [8, 8192, 6144], P('dp', 'tensor')
Inputs may be any that keep to these rules, and one draw needn't show every extreme that they name: `acts`: activations with feature scales that differ by column. `residue`: error memory with row and column scales that differ.
All inputs are finite; a program needn't handle non-finite values.
Results may differ from a plain program's by a relative error of at most 0.00055.
Values may be sent and summed in bfloat16 or wider, within the bound.
A program may use at most 128 MiB of HBM per device.

v0:
```python
import jax
import jax.numpy as jnp
from jax import lax
from jax.sharding import PartitionSpec as P

D_IN = 8192


highest = lax.Precision.HIGHEST


def shards(acts, grad_out, weight, residue, start_q):
    gathered = lax.all_gather(grad_out, "tensor", axis=0, tiled=True)
    grad_in = lax.dot_general(
        gathered, weight, (((1,), (1,)), ((), ())), preferred_element_type=jnp.float32
    ).astype(jnp.bfloat16)
    wgrad = lax.dot_general(
        acts, gathered, (((0,), (0,)), ((), ())), preferred_element_type=jnp.float32
    )
    replicas = lax.axis_size("dp")
    merged = wgrad + residue[0].astype(jnp.float32)
    sketch = lax.psum(jnp.dot(merged, start_q, precision=highest), "dp") / replicas
    width_in = D_IN
    rank_count = sketch.shape[1]

    def orthogonal_step(index, basis):
        column = lax.dynamic_slice_in_dim(sketch, index, 1, 1)[:, 0]
        coeffs = jnp.dot(basis.T, column, precision=highest)
        square = jnp.sum(column * column)
        coeffs, square = lax.psum((coeffs, square), "tensor")
        remain = column - jnp.dot(basis, coeffs, precision=highest) / width_in
        length_sq = square - jnp.sum(coeffs * coeffs) / width_in
        fresh = remain * jnp.sqrt(width_in / length_sq)
        return lax.dynamic_update_slice_in_dim(basis, fresh[:, None], index, 1)

    p_factor = lax.fori_loop(0, rank_count, orthogonal_step, jnp.zeros(sketch.shape, jnp.float32))
    local_q = lax.dot_general(
        merged,
        p_factor,
        (((0,), (0,)), ((), ())),
        precision=highest,
        preferred_element_type=jnp.float32,
    )
    scale_root = float(width_in) ** 0.5
    q_total = lax.psum(local_q, ("dp", "tensor"))
    q_factor = q_total / (replicas * scale_root)
    approx = jnp.dot(p_factor, q_factor.T, precision=highest) / scale_root
    new_residue = (merged - approx).astype(jnp.bfloat16)[None]
    return (grad_in, p_factor, q_factor, new_residue)


def solution(mesh):
    in_specs = (
        P("dp", "tensor"),
        P(("dp", "tensor"), None),
        P("tensor", None),
        P("dp", "tensor", None),
        P(),
    )
    out_specs = (P("dp", "tensor"), P("tensor", None), P(), P("dp", "tensor", None))
    return jax.shard_map(shards, mesh=mesh, in_specs=in_specs, out_specs=out_specs, check_vma=False)
```

profile of v0, /device:TPU:1, one launch (start us, length us, event | category | flops | bytes accessed | tf_op | source)
XLA Modules:
  0.0 1556.9 jit_solution(8946782508275386679)
XLA Ops:
  8.0 97.0 %all-gather.2.cloned.1.call-done = bf16[1024,6144]{1,0:T(8,128)(2,1)} async-done(((bf16[64,6144]{1,0:T(8,128)(2,1)}), bf16[1024,6144]{1,0:T(8,128)(2,1)}) %all-gather.2.cloned.1.call-update) | async-done | bytes 12582928 | tf_op jit(solution)/shard_map/all_gather | solution.py:13
  133.1 65.5 %all-reduce.6.cloned.1.call-done = f32[512,32]{0,1:T(8,128)} async-done(((f32[512,32]{0,1:T(8,128)}), f32[512,32]{0,1:T(8,128)}) %all-reduce.6.cloned.1.call-update) | async-done | bytes 65552 | tf_op jit(solution)/shard_map/psum | solution.py:22
  199.4 1181.8 %while.13 = (s32[]{:T(128)}, f32[512,32]{0,1:T(8,128)S(1)}, f32[512,32]{0,1:T(8,128)S(1)}, s32[]{:T(128)}, f32[]{:T(128)}, /*index=5*/f32[]{:T(128)}, s32[]{:T(128)}) while((s32[]{:T(128)}, f32[512,32]{0,1:T(8,128)S(1)}, f32[512,32]{0,1:T(8,128)S(1)}, s32[]{:T(128)}, f32[]{:T(128)}, /*index=5*/f32[]{:T(128)}, s32[]{:T(128)}) %tuple.34), condition=%wide.region_6.0_spmd, body=%wide.region_1.0_spmd.sunk | while | flops 395876 | bytes 152349 | solution.py:36
  200.2 38.7 %all-reduce.2 = (f32[32]{0:T(128)S(1)}, f32[]{:T(128)}) all-reduce(f32[32]{0:T(128)S(1)} %convolution_bitcast_fusion.2, f32[]{:T(128)} %multiply_reduce_fusion.4), channel_id=1, replica_groups=mesh['dp'=8,'tensor'=16] {'tensor'}, use_global_device_ids=true, to_apply=%region_2.0 | all-reduce | flops 33 | bytes 264 | tf_op jit(solution)/shard_map/while/body/eval_jaxpr/psum | solution.py:30
  241.9 33.8 %all-reduce.2 = (f32[32]{0:T(128)S(1)}, f32[]{:T(128)}) all-reduce(f32[32]{0:T(128)S(1)} %convolution_bitcast_fusion.2, f32[]{:T(128)} %multiply_reduce_fusion.4), channel_id=1, replica_groups=mesh['dp'=8,'tensor'=16] {'tensor'}, use_global_device_ids=true, to_apply=%region_2.0 | all-reduce | flops 33 | bytes 264 | tf_op jit(solution)/shard_map/while/body/eval_jaxpr/psum | solution.py:30
  315.4 33.8 %all-reduce.2 = (f32[32]{0:T(128)S(1)}, f32[]{:T(128)}) all-reduce(f32[32]{0:T(128)S(1)} %convolution_bitcast_fusion.2, f32[]{:T(128)} %multiply_reduce_fusion.4), channel_id=1, replica_groups=mesh['dp'=8,'tensor'=16] {'tensor'}, use_global_device_ids=true, to_apply=%region_2.0 | all-reduce | flops 33 | bytes 264 | tf_op jit(solution)/shard_map/while/body/eval_jaxpr/psum | solution.py:30
  352.2 33.8 %all-reduce.2 = (f32[32]{0:T(128)S(1)}, f32[]{:T(128)}) all-reduce(f32[32]{0:T(128)S(1)} %convolution_bitcast_fusion.2, f32[]{:T(128)} %multiply_reduce_fusion.4), channel_id=1, replica_groups=mesh['dp'=8,'tensor'=16] {'tensor'}, use_global_device_ids=true, to_apply=%region_2.0 | all-reduce | flops 33 | bytes 264 | tf_op jit(solution)/shard_map/while/body/eval_jaxpr/psum | solution.py:30
  389.0 33.8 %all-reduce.2 = (f32[32]{0:T(128)S(1)}, f32[]{:T(128)}) all-reduce(f32[32]{0:T(128)S(1)} %convolution_bitcast_fusion.2, f32[]{:T(128)} %multiply_reduce_fusion.4), channel_id=1, replica_groups=mesh['dp'=8,'tensor'=16] {'tensor'}, use_global_device_ids=true, to_apply=%region_2.0 | all-reduce | flops 33 | bytes 264 | tf_op jit(solution)/shard_map/while/body/eval_jaxpr/psum | solution.py:30
  425.8 33.8 %all-reduce.2 = (f32[32]{0:T(128)S(1)}, f32[]{:T(128)}) all-reduce(f32[32]{0:T(128)S(1)} %convolution_bitcast_fusion.2, f32[]{:T(128)} %multiply_reduce_fusion.4), channel_id=1, replica_groups=mesh['dp'=8,'tensor'=16] {'tensor'}, use_global_device_ids=true, to_apply=%region_2.0 | all-reduce | flops 33 | bytes 264 | tf_op jit(solution)/shard_map/while/body/eval_jaxpr/psum | solution.py:30
  462.5 33.8 %all-reduce.2 = (f32[32]{0:T(128)S(1)}, f32[]{:T(128)}) all-reduce(f32[32]{0:T(128)S(1)} %convolution_bitcast_fusion.2, f32[]{:T(128)} %multiply_reduce_fusion.4), channel_id=1, replica_groups=mesh['dp'=8,'tensor'=16] {'tensor'}, use_global_device_ids=true, to_apply=%region_2.0 | all-reduce | flops 33 | bytes 264 | tf_op jit(solution)/shard_map/while/body/eval_jaxpr/psum | solution.py:30
  536.1 33.8 %all-reduce.2 = (f32[32]{0:T(128)S(1)}, f32[]{:T(128)}) all-reduce(f32[32]{0:T(128)S(1)} %convolution_bitcast_fusion.2, f32[]{:T(128)} %multiply_reduce_fusion.4), channel_id=1, replica_groups=mesh['dp'=8,'tensor'=16] {'tensor'}, use_global_device_ids=true, to_apply=%region_2.0 | all-reduce | flops 33 | bytes 264 | tf_op jit(solution)/shard_map/while/body/eval_jaxpr/psum | solution.py:30
  572.9 33.8 %all-reduce.2 = (f32[32]{0:T(128)S(1)}, f32[]{:T(128)}) all-reduce(f32[32]{0:T(128)S(1)} %convolution_bitcast_fusion.2, f32[]{:T(128)} %multiply_reduce_fusion.4), channel_id=1, replica_groups=mesh['dp'=8,'tensor'=16] {'tensor'}, use_global_device_ids=true, to_apply=%region_2.0 | all-reduce | flops 33 | bytes 264 | tf_op jit(solution)/shard_map/while/body/eval_jaxpr/psum | solution.py:30
  683.2 33.8 %all-reduce.2 = (f32[32]{0:T(128)S(1)}, f32[]{:T(128)}) all-reduce(f32[32]{0:T(128)S(1)} %convolution_bitcast_fusion.2, f32[]{:T(128)} %multiply_reduce_fusion.4), channel_id=1, replica_groups=mesh['dp'=8,'tensor'=16] {'tensor'}, use_global_device_ids=true, to_apply=%region_2.0 | all-reduce | flops 33 | bytes 264 | tf_op jit(solution)/shard_map/while/body/eval_jaxpr/psum | solution.py:30
  720.0 33.8 %all-reduce.2 = (f32[32]{0:T(128)S(1)}, f32[]{:T(128)}) all-reduce(f32[32]{0:T(128)S(1)} %convolution_bitcast_fusion.2, f32[]{:T(128)} %multiply_reduce_fusion.4), channel_id=1, replica_groups=mesh['dp'=8,'tensor'=16] {'tensor'}, use_global_device_ids=true, to_apply=%region_2.0 | all-reduce | flops 33 | bytes 264 | tf_op jit(solution)/shard_map/while/body/eval_jaxpr/psum | solution.py:30
  830.3 33.8 %all-reduce.2 = (f32[32]{0:T(128)S(1)}, f32[]{:T(128)}) all-reduce(f32[32]{0:T(128)S(1)} %convolution_bitcast_fusion.2, f32[]{:T(128)} %multiply_reduce_fusion.4), channel_id=1, replica_groups=mesh['dp'=8,'tensor'=16] {'tensor'}, use_global_device_ids=true, to_apply=%region_2.0 | all-reduce | flops 33 | bytes 264 | tf_op jit(solution)/shard_map/while/body/eval_jaxpr/psum | solution.py:30
  867.1 33.8 %all-reduce.2 = (f32[32]{0:T(128)S(1)}, f32[]{:T(128)}) all-reduce(f32[32]{0:T(128)S(1)} %convolution_bitcast_fusion.2, f32[]{:T(128)} %multiply_reduce_fusion.4), channel_id=1, replica_groups=mesh['dp'=8,'tensor'=16] {'tensor'}, use_global_device_ids=true, to_apply=%region_2.0 | all-reduce | flops 33 | bytes 264 | tf_op jit(solution)/shard_map/while/body/eval_jaxpr/psum | solution.py:30
  940.7 33.8 %all-reduce.2 = (f32[32]{0:T(128)S(1)}, f32[]{:T(128)}) all-reduce(f32[32]{0:T(128)S(1)} %convolution_bitcast_fusion.2, f32[]{:T(128)} %multiply_reduce_fusion.4), channel_id=1, replica_groups=mesh['dp'=8,'tensor'=16] {'tensor'}, use_global_device_ids=true, to_apply=%region_2.0 | all-reduce | flops 33 | bytes 264 | tf_op jit(solution)/shard_map/while/body/eval_jaxpr/psum | solution.py:30
  977.4 33.8 %all-reduce.2 = (f32[32]{0:T(128)S(1)}, f32[]{:T(128)}) all-reduce(f32[32]{0:T(128)S(1)} %convolution_bitcast_fusion.2, f32[]{:T(128)} %multiply_reduce_fusion.4), channel_id=1, replica_groups=mesh['dp'=8,'tensor'=16] {'tensor'}, use_global_device_ids=true, to_apply=%region_2.0 | all-reduce | flops 33 | bytes 264 | tf_op jit(solution)/shard_map/while/body/eval_jaxpr/psum | solution.py:30
  1014.2 33.8 %all-reduce.2 = (f32[32]{0:T(128)S(1)}, f32[]{:T(128)}) all-reduce(f32[32]{0:T(128)S(1)} %convolution_bitcast_fusion.2, f32[]{:T(128)} %multiply_reduce_fusion.4), channel_id=1, replica_groups=mesh['dp'=8,'tensor'=16] {'tensor'}, use_global_device_ids=true, to_apply=%region_2.0 | all-reduce | flops 33 | bytes 264 | tf_op jit(solution)/shard_map/while/body/eval_jaxpr/psum | solution.py:30
  1087.8 33.8 %all-reduce.2 = (f32[32]{0:T(128)S(1)}, f32[]{:T(128)}) all-reduce(f32[32]{0:T(128)S(1)} %convolution_bitcast_fusion.2, f32[]{:T(128)} %multiply_reduce_fusion.4), channel_id=1, replica_groups=mesh['dp'=8,'tensor'=16] {'tensor'}, use_global_device_ids=true, to_apply=%region_2.0 | all-reduce | flops 33 | bytes 264 | tf_op jit(solution)/shard_map/while/body/eval_jaxpr/psum | solution.py:30
  1124.5 33.8 %all-reduce.2 = (f32[32]{0:T(128)S(1)}, f32[]{:T(128)}) all-reduce(f32[32]{0:T(128)S(1)} %convolution_bitcast_fusion.2, f32[]{:T(128)} %multiply_reduce_fusion.4), channel_id=1, replica_groups=mesh['dp'=8,'tensor'=16] {'tensor'}, use_global_device_ids=true, to_apply=%region_2.0 | all-reduce | flops 33 | bytes 264 | tf_op jit(solution)/shard_map/while/body/eval_jaxpr/psum | solution.py:30
  1234.9 33.8 %all-reduce.2 = (f32[32]{0:T(128)S(1)}, f32[]{:T(128)}) all-reduce(f32[32]{0:T(128)S(1)} %convolution_bitcast_fusion.2, f32[]{:T(128)} %multiply_reduce_fusion.4), channel_id=1, replica_groups=mesh['dp'=8,'tensor'=16] {'tensor'}, use_global_device_ids=true, to_apply=%region_2.0 | all-reduce | flops 33 | bytes 264 | tf_op jit(solution)/shard_map/while/body/eval_jaxpr/psum | solution.py:30
  1271.7 33.8 %all-reduce.2 = (f32[32]{0:T(128)S(1)}, f32[]{:T(128)}) all-reduce(f32[32]{0:T(128)S(1)} %convolution_bitcast_fusion.2, f32[]{:T(128)} %multiply_reduce_fusion.4), channel_id=1, replica_groups=mesh['dp'=8,'tensor'=16] {'tensor'}, use_global_device_ids=true, to_apply=%region_2.0 | all-reduce | flops 33 | bytes 264 | tf_op jit(solution)/shard_map/while/body/eval_jaxpr/psum | solution.py:30
  1405.0 129.5 %all-reduce.8.cloned.1.call-done = f32[6144,32]{0,1:T(8,128)} async-done(((f32[6144,32]{0,1:T(8,128)}), f32[6144,32]{0,1:T(8,128)}) %all-reduce.8.cloned.1.call-update) | async-done | bytes 786448 | tf_op jit(solution)/shard_map/psum | solution.py:45
  (260 shorter events, 524.7 us)
Async XLA Ops:
  7.2 97.8 %copy-start = (bf16[1024,512]{1,0:T(8,128)(2,1)S(1)}, bf16[1024,512]{1,0:T(8,128)(2,1)}, u32[]{:S(2)}) copy-start(bf16[1024,512]{1,0:T(8,128)(2,1)} %param.7) | copy-start | bytes 3145732
  7.2 97.8 %all-gather.2.cloned.1.call-start = ((), (), s32[]{:S(2)}) async-start(), calls=%async_computation | async-start | bytes 13369344 | tf_op jit(solution)/shard_map/all_gather | solution.py:13
  7.9 112.8 %copy-start.4 = (f32[6144,32]{0,1:T(8,128)S(1)}, f32[6144,32]{0,1:T(8,128)}, u32[]{:S(2)}) copy-start(f32[6144,32]{0,1:T(8,128)} %param.11) | copy-start | bytes 2359300
  7.9 190.6 %all-reduce.6.cloned.1.call-start = ((), (), s32[]{:S(2)}) async-start(), calls=%async_computation.1 | async-start | bytes 131072 | tf_op jit(solution)/shard_map/psum | solution.py:22
  116.2 4.6 copy-start.1
  132.9 1401.6 %all-reduce.8.cloned.1.call-start = ((), (), s32[]{:S(2)}) async-start(), calls=%async_computation.2 | async-start | bytes 1572864 | tf_op jit(solution)/shard_map/psum | solution.py:45
  1381.2 154.5 %copy-start.2 = (f32[512,32]{0,1:T(8,128)}, f32[512,32]{0,1:T(8,128)S(1)}, u32[]{:S(2)}) copy-start(f32[512,32]{0,1:T(8,128)S(1)} %get-tuple-element.73) | copy-start | bytes 196612
  1535.7 14.6 copy-start.3
Sparse Core Ops, SparseCore 0:
  10.4 94.4 all-gather.1
  133.0 65.5 all-reduce.5
  1392.8 141.6 all-reduce.7
where the time goes:
time: 1560 us
  blocking collectives  1090 us (70%)
  waiting for transfers between devices  293 us (19%)
  matrix products  70.8 us (5%)
  loops' own time  45.3 us (3%)
  other arithmetic  40.7 us (3%)
    psum x32, blocking collectives, orthogonal_step(): coeffs, square = lax.psum((coeffs, square), 'tensor')  1090 us
    psum x1, waiting for transfers between devices, shards(): q_total = lax.psum(local_q, ('dp', 'tensor'))  129 us
    all_gather x1, waiting for transfers between devices, shards(): gathered = lax.all_gather(grad_out, 'tensor', axis=0, tiled=True)  97 us
    psum x1, waiting for transfers between devices, shards(): lax.psum(jnp.dot(merged, start_q, precision=highest), 'dp') / replicas  65.5 us
    another operation x1, loops' own time, shards(): lax.fori_loop(0, rank_count, orthogonal_step, jnp.zeros(sketch.shape, jnp...  45.3 us
  transfers between devices with their start and end apart: 3, of which 3 were waited for; matrix products, arithmetic and copies ran while one was open for 1% of the time, Pallas kernels for 0%

commit v1 on v0

v1 whole, which is shorter than its diff:
```python
import math

import jax
import jax.numpy as jnp
from jax import lax
from jax.experimental import pallas as pl
from jax.experimental.pallas import tpu as pltpu
from jax.sharding import PartitionSpec as P

MESH = pl.DeviceIdType.MESH
F32, BF16 = jnp.float32, jnp.bfloat16

D_IN, D_OUT, RANK, REPLICAS = 8192, 6144, 32, 8
TOK, FEAT, OWN = 1024, 512, 64
CW = 512
NC = D_OUT // CW
NT = (((1,), (1,)), ((), ()))

STAGE_AT = dict(a=1, b=2, c=3, d=4, e=5, f=6, g=7, h=8, i=9, j=10)


def place():
    d, t = lax.axis_index("dp"), lax.axis_index("tensor")
    return dict(y_lo=d // 4, z=d % 4, x=t // 4, y_hi=(t // 2) % 2, core=t % 2)


def device(at, **moved):
    q = {**at, **moved}
    return {"dp": q["y_lo"] * 4 + q["z"], "tensor": q["x"] * 4 + q["y_hi"] * 2 + q["core"]}


def along_y(at, by):
    y = (at["y_hi"] * 2 + at["y_lo"] + by) % 4
    return device(at, y_hi=y // 2, y_lo=y % 2)


def split3(v):
    hi = v.astype(BF16)
    rest = v - hi.astype(F32)
    mid = rest.astype(BF16)
    low = (rest - mid.astype(F32)).astype(BF16)
    return hi, mid, low


def rows3(v):
    return jnp.concatenate(split3(v), axis=0)


def sum3(v):
    n = v.shape[0] // 3
    return v[:n] + (v[n : 2 * n] + v[2 * n :])


def dot(a, b, dims=(((1,), (0,)), ((), ()))):
    return lax.dot_general(a, b, dims, preferred_element_type=F32)


def kernel(
    acts_hbm, grad_hbm, weight_hbm, residue_hbm, qt_hbm,
    gin_hbm, pt_ref, qt_out_ref, new_hbm,
    g, weight, residue, merged, acts, acts_t, gin, gin_out, stage,
    qt, qt3, gq, gq3, part, sk_z, sk_y, st, st3, z_out, z_in, gram_in, gram_core, linv,
    b_own, b_core, b_z, piece_z, b_y, piece_y, b_x, q_all, b_t, q6, p6,
    load_sem, bulk_send, bulk_recv, core_send, core_recv, own_sem,
    gq_send, gq_recv, z_send, z_recv, gr_send, gr_recv, ring_send, ring_recv, pair_send, pair_recv, out_sem,
):
    at = place()
    x, y_hi, y_lo, z, core = at["x"], at["y_hi"], at["y_lo"], at["z"], at["core"]
    y = y_hi * 2 + y_lo
    me = x * 4 + y_hi * 2 + core
    chip = x * 2 + y_hi
    other = device(at, core=1 - core)
    peers = [(dx, dy) for dx in range(4) for dy in range(2) if (dx, dy) != (0, 0)]
    peer_ids = [device(at, x=(x + dx) % 4, y_hi=(y_hi + dy) % 2) for dx, dy in peers]
    ring = {
        "x": [device(at, x=(x + i) % 4) for i in (1, 2, 3)],
        "y": [along_y(at, i) for i in (1, 2, 3)],
        "z": [device(at, z=(z + i) % 4) for i in (1, 2, 3)],
    }

    def own_rows(dx, dy):
        t = ((x + dx + 4) % 4) * 4 + ((y_hi + dy) % 2) * 2 + core
        return pl.ds(pl.multiple_of(t * OWN, OWN), OWN)

    mine = own_rows(0, 0)
    chip_rows = pl.ds(pl.multiple_of(chip * 2 * OWN, 2 * OWN), 2 * OWN)

    def chunk(k):
        return pl.ds(pl.multiple_of(k * CW, CW), CW)

    for k in range(NC):
        pltpu.make_async_copy(
            grad_hbm.at[:, pl.ds(k * CW, CW)], g.at[k, mine], load_sem.at[0]
        ).start()
    load_q = pltpu.make_async_copy(qt_hbm, qt, load_sem.at[1])
    load_res = pltpu.make_async_copy(residue_hbm, residue, load_sem.at[2])
    load_acts = pltpu.make_async_copy(acts_hbm, acts, load_sem.at[3])
    load_w = pltpu.make_async_copy(weight_hbm, weight, load_sem.at[4])
    load_q.start()
    load_acts.start()
    load_res.start()
    load_w.start()

    barrier = pltpu.get_barrier_semaphore()
    greet = [*peer_ids, other, ring["y"][0], ring["y"][2], *ring["z"]]
    for who in greet:
        pl.semaphore_signal(barrier, inc=1, device_id=who, device_id_type=MESH)
    pl.semaphore_wait(barrier, len(greet))

    def remote(src, dst, send, recv, who):
        return pltpu.make_async_remote_copy(
            src_ref=src, dst_ref=dst, send_sem=send, recv_sem=recv, device_id=who, device_id_type=MESH
        )

    def bulk(flow, k, rows, who):
        block = g.at[k, rows]
        return remote(block, block, bulk_send.at[flow], bulk_recv.at[flow, k], who)

    def arrived(flow, k):
        bulk(flow, k, mine, other).wait_recv()

    def to_core(k, rows):
        block = g.at[k, rows]
        remote(block, block, core_send.at[0], core_recv.at[k], other).start()

    right, left, across = ring["x"][0], ring["x"][2], device(at, y_hi=1 - y_hi)

    pltpu.make_async_copy(g.at[:, mine], g.at[:, mine], load_sem.at[0]).wait()
    own_copy = remote(g.at[:, mine], g.at[:, mine], own_sem.at[0], own_sem.at[1], other)
    own_copy.start()
    load_q.wait()
    qt3[...] = rows3(qt[...])

    def step(s, carry):
        @pl.when(s < NC)
        def _():
            bulk(0, s, mine, right).start()
            bulk(1, s, mine, left).start()
            bulk(2, s, mine, across).start()

        @pl.when(s == 0)
        def _():
            own_copy.wait_recv()
            total = jnp.zeros((3 * RANK, 2 * OWN), F32)
            for k in range(NC):
                total += dot(qt3[:, k * CW : (k + 1) * CW], g[k, chip_rows, :], NT)
            gq[chip] = sum3(total)
            for i, who in enumerate(peer_ids):
                remote(gq.at[chip], gq.at[chip], gq_send.at[i], gq_recv.at[i], who).start()
            load_res.wait()

            def add(k, total):
                return total + dot(qt3[:, chunk(k)], residue[:, chunk(k)], NT)

            part[...] = sum3(lax.fori_loop(0, NC, add, jnp.zeros((3 * RANK, FEAT), F32)))
            load_acts.wait()
            acts_t[...] = acts[...].T
            gin[...] = jnp.zeros_like(gin)

        @pl.when((s >= 1) & (s <= NC))
        def _():
            k = s - 1
            arrived(0, k)
            arrived(1, k)
            odd = k % 2
            ahead = device(at, x=(x + 1 + 2 * odd) % 4)
            bulk(3, k, own_rows(2 * odd - 1, 0), ahead).start()
            arrived(2, k)
            bulk(4, k, own_rows(0, 1), right).start()
            bulk(5, k, own_rows(0, 1), left).start()
            to_core(k, own_rows(-1, 0))
            to_core(k, own_rows(1, 0))
            to_core(k, own_rows(0, 1))

        @pl.when((s >= 2) & (s <= NC + 1))
        def _():
            k = s - 2
            arrived(3, k)
            bulk(6, k, own_rows(2, 0), across).start()
            to_core(k, own_rows(2, 0))
            arrived(4, k)
            to_core(k, own_rows(-1, 1))
            arrived(5, k)
            to_core(k, own_rows(1, 1))

        @pl.when((s >= 3) & (s <= NC + 2))
        def _():
            k = s - 3
            arrived(6, k)
            to_core(k, own_rows(2, 1))

        @pl.when(s == 4)
        def _():
            load_w.wait()

        @pl.when(s >= 4)
        def _():
            k = s - 4
            landed = g.at[k, pl.ds(0, 7 * OWN)]
            remote(landed, landed, core_send.at[0], core_recv.at[k], other).wait_recv()
            merged[k] = dot(acts_t[...], g[k]) + residue[:, chunk(k)].astype(F32)
            gin[...] += dot(g[k], weight[:, chunk(k)], NT)

        def stage_at(name):
            return pl.when(s == STAGE_AT[name])

        @stage_at("a")
        def _():
            for i, who in enumerate(peer_ids):
                remote(gq.at[chip], gq.at[chip], gq_send.at[i], gq_recv.at[i], who).wait()
            for j in range(8):
                gq3[:, j * 128 : (j + 1) * 128] = rows3(gq[j])
            sk_z[z] = part[...] + sum3(dot(gq3[...], acts[...]))
            for i, who in enumerate(ring["z"]):
                remote(sk_z.at[z], sk_z.at[z], ring_send.at[0, i], ring_recv.at[0, i], who).start()

        @stage_at("b")
        def _():
            for i, who in enumerate(ring["z"]):
                remote(sk_z.at[z], sk_z.at[z], ring_send.at[0, i], ring_recv.at[0, i], who).wait()
            sk_y[y_lo] = (sk_z[0] + sk_z[1]) + (sk_z[2] + sk_z[3])
            remote(sk_y.at[y_lo], sk_y.at[y_lo], pair_send.at[0], pair_recv.at[0], device(at, y_lo=1 - y_lo)).start()

        @stage_at("c")
        def _():
            remote(sk_y.at[y_lo], sk_y.at[y_lo], pair_send.at[0], pair_recv.at[0], device(at, y_lo=1 - y_lo)).wait()
            sketch = (sk_y[0] + sk_y[1]) * (1.0 / REPLICAS)
            st[...] = sketch
            st3[...] = rows3(sketch)
            zt = sum3(dot(st3[...], acts_t[...]))
            for j in range(8):
                z_out[j] = zt[:, j * 128 : (j + 1) * 128]
            for i, who in enumerate(peer_ids):
                dx, dy = peers[i]
                there = ((x + dx) % 4) * 2 + (y_hi + dy) % 2
                remote(z_out.at[there], z_in.at[chip], z_send.at[i], z_recv.at[i], who).start()
            z_in[chip] = z_out[chip]
            gram_in[chip] = jnp.zeros((RANK, 128), F32)
            gram_in[chip, :, 0:RANK] = lax.dot_general(
                sketch, sketch, NT, precision=lax.Precision.HIGHEST, preferred_element_type=F32
            )
            for i, who in enumerate(peer_ids):
                remote(gram_in.at[chip], gram_in.at[chip], gr_send.at[i], gr_recv.at[i], who).start()

            def from_residue(k, _):
                r = sum3(dot(st3[...], residue[:, chunk(k)]))
                for i in range(CW // 128):
                    b_own[2 * (k * 4 + i)] = r[0:16, i * 128 : (i + 1) * 128]
                    b_own[2 * (k * 4 + i) + 1] = r[16:32, i * 128 : (i + 1) * 128]
                return 0

            lax.fori_loop(0, NC, from_residue, 0)

        half = pl.ds(core * 48, 48)
        half_there = pl.ds((1 - core) * 48, 48)

        @stage_at("d")
        def _():
            for i, who in enumerate(peer_ids):
                remote(z_out.at[0], z_in.at[0], z_send.at[i], z_recv.at[i], who).wait()
            total = z_in[0]
            for j in range(1, 8):
                total = total + z_in[j]
            z3 = rows3(total)

            def from_grad(k, _):
                r = sum3(dot(z3, g[k, chip_rows, :]))
                for i in range(CW // 128):
                    b_own[2 * (k * 4 + i)] += r[0:16, i * 128 : (i + 1) * 128]
                    b_own[2 * (k * 4 + i) + 1] += r[16:32, i * 128 : (i + 1) * 128]
                return 0

            lax.fori_loop(0, NC, from_grad, 0)
            remote(b_own.at[half_there], b_core, pair_send.at[1], pair_recv.at[1], other).start()
            for i, who in enumerate(peer_ids):
                remote(gram_in.at[chip], gram_in.at[chip], gr_send.at[i], gr_recv.at[i], who).wait()
            total = gram_in[0]
            for j in range(1, 8):
                total = total + gram_in[j]
            gram_core[core] = total
            remote(gram_core.at[core], gram_core.at[core], pair_send.at[2], pair_recv.at[2], other).start()

        @stage_at("e")
        def _():
            remote(b_own.at[half_there], b_core, pair_send.at[1], pair_recv.at[1], other).wait()
            b_core[...] += b_own[half]
            for i, who in enumerate(ring["z"]):
                there = pl.ds(((z + i + 1) % 4) * 12, 12)
                remote(b_core.at[there], b_z.at[i], ring_send.at[1, i], ring_recv.at[1, i], who).start()
            remote(gram_core.at[core], gram_core.at[core], pair_send.at[2], pair_recv.at[2], other).wait()
            gram = (gram_core[0] + gram_core[1]) * (1.0 / D_IN)
            sub = lax.broadcasted_iota(jnp.int32, (RANK, 128), 0)
            lane = lax.broadcasted_iota(jnp.int32, (RANK, 128), 1)
            unit = jnp.where(sub == lane, 1.0, 0.0).astype(F32)

            def eliminate(j, both):
                a, e = both
                row_a = jnp.sum(jnp.where(sub == j, a, 0.0), axis=0, keepdims=True)
                row_e = jnp.sum(jnp.where(sub == j, e, 0.0), axis=0, keepdims=True)
                col = jnp.sum(jnp.where(lane == j, a, 0.0), axis=1, keepdims=True)
                diag = jnp.sum(jnp.where(lane[0:1] == j, row_a, 0.0), axis=1, keepdims=True)
                scale = 1.0 / jnp.sqrt(diag)
                row_a, row_e = row_a * scale, row_e * scale
                factor = jnp.where(sub > j, col * scale, 0.0)
                a = jnp.where(sub == j, row_a, a - factor * row_a)
                e = jnp.where(sub == j, row_e, e - factor * row_e)
                return a, e

            linv[...] = lax.fori_loop(0, RANK, eliminate, (gram, unit))[1]

        @stage_at("f")
        def _():
            for i, who in enumerate(ring["z"]):
                remote(b_z.at[i], b_z.at[i], ring_send.at[1, i], ring_recv.at[1, i], who).wait()
            piece_z[...] = (b_core[pl.ds(z * 12, 12)] + b_z[0]) + (b_z[1] + b_z[2])
            for i, who in enumerate(ring["y"]):
                there = pl.ds(((y + i + 1) % 4) * 3, 3)
                remote(piece_z.at[there], b_y.at[i], ring_send.at[2, i], ring_recv.at[2, i], who).start()

        @stage_at("g")
        def _():
            for i, who in enumerate(ring["y"]):
                remote(b_y.at[i], b_y.at[i], ring_send.at[2, i], ring_recv.at[2, i], who).wait()
            b_x[x] = (piece_z[pl.ds(y * 3, 3)] + b_y[0]) + (b_y[1] + b_y[2])
            for i, who in enumerate(ring["x"]):
                remote(b_x.at[x], b_x.at[x], ring_send.at[3, i], ring_recv.at[3, i], who).start()

        piece = pl.ds(core * 48 + z * 12 + y * 3, 3)
        pieces = pl.ds(core * 48 + z * 12, 12)

        @stage_at("h")
        def _():
            for i, who in enumerate(ring["x"]):
                remote(b_x.at[x], b_x.at[x], ring_send.at[3, i], ring_recv.at[3, i], who).wait()
            q_all[piece] = (b_x[0] + b_x[1]) + (b_x[2] + b_x[3])
            for i, who in enumerate(ring["y"]):
                remote(q_all.at[piece], q_all.at[piece], ring_send.at[4, i], ring_recv.at[4, i], who).start()

        @stage_at("i")
        def _():
            for i, who in enumerate(ring["y"]):
                remote(q_all.at[piece], q_all.at[piece], ring_send.at[4, i], ring_recv.at[4, i], who).wait()
            for i, who in enumerate(ring["z"]):
                remote(q_all.at[pieces], q_all.at[pieces], ring_send.at[5, i], ring_recv.at[5, i], who).start()

        @stage_at("j")
        def _():
            for i, who in enumerate(ring["z"]):
                remote(q_all.at[pieces], q_all.at[pieces], ring_send.at[5, i], ring_recv.at[5, i], who).wait()
            remote(q_all.at[half], q_all.at[half], pair_send.at[3], pair_recv.at[3], other).start()

        return carry

    lax.fori_loop(0, NC + 4, step, 0)

    gin_out[...] = gin[...].astype(BF16)
    store_gin = pltpu.make_async_copy(gin_out, gin_hbm, out_sem.at[2])
    store_gin.start()

    inverse = linv[:, 0:RANK]
    ih, im, il = split3(inverse)
    i6 = jnp.concatenate([ih, ih, im, ih, il, im], axis=1)

    def stack6(v):
        h, m, low = split3(v)
        return jnp.concatenate([h, m, h, low, h, m], axis=0)

    p_t = dot(i6, stack6(st[...]))
    pt_ref[...] = p_t
    ph, pm, pw = split3(p_t)
    p6[...] = jnp.concatenate([ph, ph, pm, ph, pw, pm], axis=0).T

    half = pl.ds(core * 48, 48)
    remote(q_all.at[half], q_all.at[half], pair_send.at[3], pair_recv.at[3], other).wait()

    def store(k, slot):
        return pltpu.make_async_copy(stage.at[slot], new_hbm.at[:, chunk(k)], out_sem.at[slot])

    def finish(k, carry):
        for i in range(CW // 128):
            b_t[0:16, i * 128 : (i + 1) * 128] = q_all[2 * (k * 4 + i)]
            b_t[16:32, i * 128 : (i + 1) * 128] = q_all[2 * (k * 4 + i) + 1]
        q_t = dot(i6, stack6(b_t[...])) * (1.0 / (REPLICAS * math.sqrt(D_IN)))
        qt_out_ref[:, chunk(k)] = q_t
        q6[...] = stack6(q_t * (1.0 / math.sqrt(D_IN)))
        slot = k % 2

        @pl.when(k >= 2)
        def _():
            store(k - 2, slot).wait()

        stage[slot] = (merged[k] - dot(p6[...], q6[...])).astype(BF16)
        store(k, slot).start()
        return carry

    lax.fori_loop(0, NC, finish, 0)
    store(NC - 2, 0).wait()
    store(NC - 1, 1).wait()
    store_gin.wait()

    own_copy.wait_send()
    for flow in range(7):
        block = g.at[:, pl.ds(0, OWN)]
        remote(block, block, bulk_send.at[flow], bulk_recv.at[flow, 0], other).wait_send()
    block = g.at[:, pl.ds(0, 7 * OWN)]
    remote(block, block, core_send.at[0], core_recv.at[0], other).wait_send()


def shards(acts, grad_out, weight, residue, start_q):
    vmem, dma = pltpu.VMEM, pltpu.SemaphoreType.DMA
    hbm = pl.BlockSpec(memory_space=pl.ANY)
    here = pl.BlockSpec(memory_space=pltpu.VMEM)
    flops = 4 * TOK * FEAT * D_OUT
    grad_in, p_t, q_t, new = pl.pallas_call(
        kernel,
        out_shape=[
            jax.ShapeDtypeStruct((TOK, FEAT), BF16),
            jax.ShapeDtypeStruct((RANK, FEAT), F32),
            jax.ShapeDtypeStruct((RANK, D_OUT), F32),
            jax.ShapeDtypeStruct((FEAT, D_OUT), BF16),
        ],
        in_specs=[hbm] * 5,
        out_specs=[hbm, here, here, hbm],
        scratch_shapes=[
            vmem((NC, TOK, CW), BF16),
            vmem((FEAT, D_OUT), BF16),
            vmem((FEAT, D_OUT), BF16),
            vmem((NC, FEAT, CW), F32),
            vmem((TOK, FEAT), BF16),
            vmem((FEAT, TOK), BF16),
            vmem((TOK, FEAT), F32),
            vmem((TOK, FEAT), BF16),
            vmem((2, FEAT, CW), BF16),
            vmem((RANK, D_OUT), F32),
            vmem((3 * RANK, D_OUT), BF16),
            vmem((8, RANK, 128), F32),
            vmem((3 * RANK, TOK), BF16),
            vmem((RANK, FEAT), F32),
            vmem((4, RANK, FEAT), F32),
            vmem((2, RANK, FEAT), F32),
            vmem((RANK, FEAT), F32),
            vmem((3 * RANK, FEAT), BF16),
            vmem((8, RANK, 128), F32),
            vmem((8, RANK, 128), F32),
            vmem((8, RANK, 128), F32),
            vmem((2, RANK, 128), F32),
            vmem((RANK, 128), F32),
            vmem((96, 16, 128), F32),
            vmem((48, 16, 128), F32),
            vmem((3, 12, 16, 128), F32),
            vmem((12, 16, 128), F32),
            vmem((3, 3, 16, 128), F32),
            vmem((3, 16, 128), F32),
            vmem((4, 3, 16, 128), F32),
            vmem((96, 16, 128), F32),
            vmem((RANK, CW), F32),
            vmem((6 * RANK, CW), BF16),
            vmem((FEAT, 6 * RANK), BF16),
            dma((5,)),
            dma((7,)),
            dma((7, NC)),
            dma((1,)),
            dma((NC,)),
            dma((2,)),
            dma((7,)),
            dma((7,)),
            dma((7,)),
            dma((7,)),
            dma((7,)),
            dma((7,)),
            dma((6, 3)),
            dma((6, 3)),
            dma((4,)),
            dma((4,)),
            dma((3,)),
        ],
        compiler_params=pltpu.CompilerParams(
            collective_id=1, has_side_effects=True, vmem_limit_bytes=60 * 2**20
        ),
        cost_estimate=pl.CostEstimate(flops=flops, bytes_accessed=24 * 2**20, transcendentals=0),
        name="gather_and_compress",
    )(acts, grad_out, weight, residue[0], start_q.T)
    return grad_in, p_t.T, q_t.T, new[None]


def solution(mesh):
    in_specs = (
        P("dp", "tensor"),
        P(("dp", "tensor"), None),
        P("tensor", None),
        P("dp", "tensor", None),
        P(),
    )
    out_specs = (P("dp", "tensor"), P("tensor", None), P(), P("dp", "tensor", None))
    return jax.shard_map(shards, mesh=mesh, in_specs=in_specs, out_specs=out_specs, check_vma=False)
```

time: 1560 us -> 101 us (0.06)
  blocking collectives: 1090 us -> 0 us
  waiting for transfers between devices: 293 us -> 0 us
  Pallas kernels: 0 us -> 88.3 us
  matrix products: 70.8 us -> 0 us
  loops' own time: 45.3 us -> 0 us
  other arithmetic: 40.7 us -> 0 us
    psum x32 -> x0, blocking collectives: 1090 us -> none  [orthogonal_step(): coeffs, square = lax.psum((coeffs, square), 'tensor')]
    psum x2 -> x0, waiting for transfers between devices: 195 us -> none  [the longest x1 129 us: shards(): q_total = lax.psum(local_q, ('dp', 'tensor'))]
    all_gather x1 -> x0, waiting for transfers between devices: 97 us -> none  [shards(): gathered = lax.all_gather(grad_out, 'tensor', axis=0, tiled=True)]
    pallas_call x0 -> x1, Pallas kernels: none -> 88.3 us  [shards(): pl.pallas_call(kernel, out_shape=[jax.ShapeDtypeStruct((TOK, FEAT), BF16)...]
    dot_general x69 -> x0, matrix products: 70.8 us -> none  [the longest x1 14.6 us: shards(): approx = jnp.dot(p_factor, q_factor.T, precision=highest) / scale_root]
    another operation x1 -> x0, loops' own time: 45.3 us -> none  [shards(): lax.fori_loop(0, rank_count, orthogonal_step, jnp.zeros(sketch.shape, jnp...]
    reduce_sum x64 -> x0, other arithmetic: 38.4 us -> none  [the longest x32 19.2 us: orthogonal_step(): square = jnp.sum(column * column)]
  transfers between devices with their start and end apart: 3 -> 0, of which waited for: 3 -> 0; matrix products, arithmetic and copies ran while one was open for 1% -> 0% of each run, Pallas kernels for 0% -> 0%
where the time goes in v1:
time: 101 us
  Pallas kernels  88.3 us (87%)
  local copies, waits for them, and re-layouts  12 us (12%)
    pallas_call x1, Pallas kernels, shards(): pl.pallas_call(kernel, out_shape=[jax.ShapeDtypeStruct((TOK, FEAT), BF16)...  88.3 us
    unnamed x4, local copies, waits for them, and re-layouts  12 us

profile of v1, /device:TPU:1, one launch (start us, length us, event | category | flops | bytes accessed | tf_op | source)
XLA Modules:
  0.0 101.0 jit_solution(15442028226141195230)
XLA Ops:
  0.6 88.3 %gather_and_compress.1 = (bf16[1024,512]{1,0:T(8,128)(2,1)}, f32[32,512]{1,0:T(8,128)}, f32[32,6144]{1,0:T(8,128)}, bf16[512,6144]{1,0:T(8,128)(2,1)}) custom-call(bf16[1024,512]{1,0:T(8,128)(2,1)} %acts_hbm.1, bf16[64,6144]{1,0:T(8,128)(2,1)} %grad_hbm.1, bf16[512,6144]{1,0:T(8,128)(2,1)} %weight_hbm.1, bf16[512,6144]{1,0:T(8,128)(2,1)} %bitcast.8, ...), custom_call_target="tpu_custom_call" | custom-call | flops 12884901888 | bytes 25165824 | tf_op jit(solution)/shard_map/gather_and_compress/pallas_call | solution.py:414
  89.0 2.3 %copy.13 = bf16[1024,512]{1,0:T(8,128)(2,1)} copy(bf16[1024,512]{1,0:T(8,128)(2,1)} %get-tuple-element.16) | data formatting | bytes 2097152
  91.3 1.5 %copy.14 = f32[512,32]{0,1:T(8,128)} copy(f32[512,32]{0,1:T(8,128)} %bitcast.7) | data formatting | bytes 131072
  92.7 2.1 %copy.15 = f32[6144,32]{0,1:T(8,128)} copy(f32[6144,32]{0,1:T(8,128)} %bitcast.6) | data formatting | bytes 1572864
  94.8 6.2 %copy.16 = bf16[1,512,6144]{2,1,0:T(8,128)(2,1)} copy(bf16[1,512,6144]{2,1,0:T(8,128)(2,1)} %bitcast.5) | data formatting | bytes 12582912

commit v2 on v1

v2 whole, which is shorter than its diff:
```python
import math

import jax
import jax.numpy as jnp
from jax import lax
from jax.experimental import pallas as pl
from jax.experimental.pallas import tpu as pltpu
from jax.sharding import PartitionSpec as P

MESH = pl.DeviceIdType.MESH
F32, BF16 = jnp.float32, jnp.bfloat16

D_IN, D_OUT, RANK, REPLICAS = 8192, 6144, 32, 8
TOK, FEAT, OWN = 1024, 512, 64
CW = 512
NC = D_OUT // CW
NT = (((1,), (1,)), ((), ()))

STAGE_AT = dict(a=1, b=3, c=4, d=5, e=8, f=7, g=8, h=9, i=10, j=11, k=12)
PARTS = 3
TILES = D_OUT // 128 * RANK // 8
PART = TILES // 2 // PARTS
STEPS = NC + 7
EARLY = 3
FINISH_FROM, FINISH_EACH = 13, 2
DONE = (STEPS - FINISH_FROM) * FINISH_EACH


def place():
    d, t = lax.axis_index("dp"), lax.axis_index("tensor")
    return dict(y_lo=d // 4, z=d % 4, x=t // 4, y_hi=(t // 2) % 2, core=t % 2)


def device(at, **moved):
    q = {**at, **moved}
    return {"dp": q["y_lo"] * 4 + q["z"], "tensor": q["x"] * 4 + q["y_hi"] * 2 + q["core"]}


def along_y(at, by):
    y = (at["y_hi"] * 2 + at["y_lo"] + by) % 4
    return device(at, y_hi=y // 2, y_lo=y % 2)


def split3(v):
    hi = v.astype(BF16)
    rest = v - hi.astype(F32)
    mid = rest.astype(BF16)
    low = (rest - mid.astype(F32)).astype(BF16)
    return hi, mid, low


def rows3(v):
    return jnp.concatenate(split3(v), axis=0)


def sum3(v):
    n = v.shape[0] // 3
    return v[:n] + (v[n : 2 * n] + v[2 * n :])


def dot(a, b, dims=(((1,), (0,)), ((), ()))):
    return lax.dot_general(a, b, dims, preferred_element_type=F32)


def kernel(
    acts_hbm, grad_hbm, weight_hbm, residue_hbm, qt_hbm,
    gin_out, pt_ref, qt_out_ref, new_ref,
    g, weight, merged, acts_t, gin,
    qt3, gq, gq3, part, sk_z, sk_y, st, st3, z_out, z_in, gram_in, gram_core, gram_all, linv, i6,
    b_own, b_core, b_z, piece_z, b_y, b_x, q_all, b_t, q6, p6,
    load_sem, bulk_send, bulk_recv, core_send, core_recv, own_sem,
    gq_send, gq_recv, z_send, z_recv, gr_send, gr_recv, ring_send, ring_recv, pair_send, pair_recv,
    bc_send, bc_recv, rs_send, rs_recv, qc_send, qc_recv,
):
    acts, qt, residue = gin_out, qt_out_ref, new_ref
    at = place()
    x, y_hi, y_lo, z, core = at["x"], at["y_hi"], at["y_lo"], at["z"], at["core"]
    y = y_hi * 2 + y_lo
    me = x * 4 + y_hi * 2 + core
    chip = x * 2 + y_hi
    other = device(at, core=1 - core)
    peers = [(dx, dy) for dx in range(4) for dy in range(2) if (dx, dy) != (0, 0)]
    peer_ids = [device(at, x=(x + dx) % 4, y_hi=(y_hi + dy) % 2) for dx, dy in peers]
    ring = {
        "x": [device(at, x=(x + i) % 4) for i in (1, 2, 3)],
        "y": [along_y(at, i) for i in (1, 2, 3)],
        "z": [device(at, z=(z + i) % 4) for i in (1, 2, 3)],
    }

    def own_rows(dx, dy):
        t = ((x + dx + 4) % 4) * 4 + ((y_hi + dy) % 2) * 2 + core
        return pl.ds(pl.multiple_of(t * OWN, OWN), OWN)

    mine = own_rows(0, 0)
    chip_rows = pl.ds(pl.multiple_of(chip * 2 * OWN, 2 * OWN), 2 * OWN)

    def chunk(k):
        return pl.ds(pl.multiple_of(k * CW, CW), CW)

    for k in range(NC):
        pltpu.make_async_copy(
            grad_hbm.at[:, pl.ds(k * CW, CW)], g.at[k, mine], load_sem.at[0]
        ).start()
    load_q = pltpu.make_async_copy(qt_hbm, qt, load_sem.at[1])
    load_res = pltpu.make_async_copy(residue_hbm, residue, load_sem.at[2])
    load_acts = pltpu.make_async_copy(acts_hbm, acts, load_sem.at[3])
    load_w = pltpu.make_async_copy(weight_hbm, weight, load_sem.at[4])
    load_q.start()
    load_acts.start()
    load_res.start()
    load_w.start()

    barrier = pltpu.get_barrier_semaphore()
    greet = [*peer_ids, other, ring["y"][0], ring["y"][2], *ring["z"]]
    for who in greet:
        pl.semaphore_signal(barrier, inc=1, device_id=who, device_id_type=MESH)
    load_q.wait()
    qt3[...] = rows3(qt[...])
    pltpu.make_async_copy(g.at[:, mine], g.at[:, mine], load_sem.at[0]).wait()
    pl.semaphore_wait(barrier, len(greet))

    def remote(src, dst, send, recv, who):
        return pltpu.make_async_remote_copy(
            src_ref=src, dst_ref=dst, send_sem=send, recv_sem=recv, device_id=who, device_id_type=MESH
        )

    def bulk(flow, k, rows, who):
        block = g.at[k, rows]
        return remote(block, block, bulk_send.at[flow], bulk_recv.at[flow, k], who)

    def arrived(flow, k):
        bulk(flow, k, mine, other).wait_recv()

    def to_core(k, rows):
        block = g.at[k, rows]
        remote(block, block, core_send.at[0], core_recv.at[k], other).start()

    right, left, across = ring["x"][0], ring["x"][2], device(at, y_hi=1 - y_hi)

    own_copy = remote(g.at[:, mine], g.at[:, mine], own_sem.at[0], own_sem.at[1], other)
    own_copy.start()

    def stack6(v):
        h, m, low = split3(v)
        return jnp.concatenate([h, m, h, low, h, m], axis=0)

    def finish(k):
        for i in range(CW // 128):
            block = q_all[pl.ds(k * (CW // 32) + 4 * i, 4)]
            b_t[:, i * 128 : (i + 1) * 128] = block.reshape(RANK, 128)
        q_t = dot(i6[...], stack6(b_t[...])) * (1.0 / (REPLICAS * math.sqrt(D_IN)))
        qt_out_ref[:, chunk(k)] = q_t
        q6[...] = stack6(q_t * (1.0 / math.sqrt(D_IN)))
        new_ref[:, chunk(k)] = (merged[k] - dot(p6[...], q6[...])).astype(BF16)

    def send_own(k):
        bulk(0, k, mine, right).start()
        bulk(1, k, mine, left).start()
        bulk(2, k, mine, across).start()

    def step(s, carry):
        @pl.when((s >= EARLY) & (s < NC))
        def _():
            send_own(s)

        @pl.when(s == 0)
        def _():
            send_own(0)
            own_copy.wait_recv()
            total = jnp.zeros((3 * RANK, 2 * OWN), F32)
            for k in range(NC):
                total += dot(qt3[:, k * CW : (k + 1) * CW], g[k, chip_rows, :], NT)
            gq[chip] = sum3(total)
            for i, who in enumerate(peer_ids):
                remote(gq.at[chip], gq.at[chip], gq_send.at[i], gq_recv.at[i], who).start()
            for k in range(1, EARLY):
                send_own(k)
            load_res.wait()

            def add(k, total):
                return total + dot(qt3[:, chunk(k)], residue[:, chunk(k)], NT)

            part[...] = sum3(lax.fori_loop(0, NC, add, jnp.zeros((3 * RANK, FEAT), F32)))
            load_acts.wait()
            acts_t[...] = acts[...].T
            gin[...] = jnp.zeros_like(gin)

        @pl.when((s >= 2) & (s < NC + 2))
        def _():
            k = s - 2
            arrived(0, k)
            arrived(1, k)
            odd = k % 2
            ahead = device(at, x=(x + 1 + 2 * odd) % 4)
            bulk(3, k, own_rows(2 * odd - 1, 0), ahead).start()
            arrived(2, k)
            bulk(4, k, own_rows(0, 1), right).start()
            bulk(5, k, own_rows(0, 1), left).start()
            to_core(k, own_rows(-1, 0))
            to_core(k, own_rows(1, 0))
            to_core(k, own_rows(0, 1))

        @pl.when((s >= 4) & (s < NC + 4))
        def _():
            k = s - 4
            arrived(3, k)
            bulk(6, k, own_rows(2, 0), across).start()
            to_core(k, own_rows(2, 0))
            arrived(4, k)
            to_core(k, own_rows(-1, 1))
            arrived(5, k)
            to_core(k, own_rows(1, 1))

        @pl.when((s >= 6) & (s < NC + 6))
        def _():
            k = s - 6
            arrived(6, k)
            to_core(k, own_rows(2, 1))

        @pl.when(s == 4)
        def _():
            load_w.wait()

        @pl.when(s >= 7)
        def _():
            k = s - 7
            landed = g.at[k, pl.ds(0, 7 * OWN)]
            remote(landed, landed, core_send.at[0], core_recv.at[k], other).wait_recv()
            merged[k] = dot(acts_t[...], g[k]) + residue[:, chunk(k)].astype(F32)
            gin[...] += dot(g[k], weight[:, chunk(k)], NT)

        def stage_at(name):
            return pl.when(s == STAGE_AT[name])

        @stage_at("a")
        def _():
            for i, who in enumerate(peer_ids):
                remote(gq.at[chip], gq.at[chip], gq_send.at[i], gq_recv.at[i], who).wait()
            for j in range(8):
                gq3[:, j * 128 : (j + 1) * 128] = rows3(gq[j])
            sk_z[z] = part[...] + sum3(dot(gq3[...], acts[...]))
            for i, who in enumerate(ring["z"]):
                remote(sk_z.at[z], sk_z.at[z], ring_send.at[0, i], ring_recv.at[0, i], who).start()

        @stage_at("b")
        def _():
            for i, who in enumerate(ring["z"]):
                remote(sk_z.at[z], sk_z.at[z], ring_send.at[0, i], ring_recv.at[0, i], who).wait()
            sk_y[y_lo] = (sk_z[0] + sk_z[1]) + (sk_z[2] + sk_z[3])
            remote(sk_y.at[y_lo], sk_y.at[y_lo], pair_send.at[0], pair_recv.at[0], device(at, y_lo=1 - y_lo)).start()

        @stage_at("c")
        def _():
            remote(sk_y.at[y_lo], sk_y.at[y_lo], pair_send.at[0], pair_recv.at[0], device(at, y_lo=1 - y_lo)).wait()
            sketch = (sk_y[0] + sk_y[1]) * (1.0 / REPLICAS)
            st[...] = sketch
            st3[...] = rows3(sketch)
            zt = sum3(dot(st3[...], acts_t[...]))
            for j in range(8):
                z_out[j] = zt[:, j * 128 : (j + 1) * 128]
            for i, who in enumerate(peer_ids):
                dx, dy = peers[i]
                there = ((x + dx) % 4) * 2 + (y_hi + dy) % 2
                remote(z_out.at[there], z_in.at[chip], z_send.at[i], z_recv.at[i], who).start()
            z_in[chip] = z_out[chip]
            gram = lax.dot_general(
                sketch, sketch, NT, precision=lax.Precision.HIGHEST, preferred_element_type=F32
            )
            for i in range(4):
                gram_in[chip, :, i * RANK : (i + 1) * RANK] = gram[i * 8 : (i + 1) * 8]
            for i, who in enumerate(peer_ids):
                remote(gram_in.at[chip], gram_in.at[chip], gr_send.at[i], gr_recv.at[i], who).start()

            def from_residue(k, _):
                r = sum3(dot(st3[...], residue[:, chunk(k)]))
                for i in range(CW // 128):
                    b_own[pl.ds(k * (CW // 32) + 4 * i, 4)] = r[:, i * 128 : (i + 1) * 128].reshape(4, 8, 128)
                return 0

            lax.fori_loop(0, NC, from_residue, 0)

        def tiles(c, h):
            return pl.ds(c * (TILES // 2) + h * PART, PART)

        def fourth(i):
            return pl.ds(i * (PART // 4), PART // 4)

        def core_copy(h, start):
            c = remote(b_own.at[tiles(1 - core, h)], b_core.at[h], bc_send.at[h], bc_recv.at[h], other)
            c.start() if start else c.wait()

        @stage_at("d")
        def _():
            for i, who in enumerate(peer_ids):
                remote(z_out.at[0], z_in.at[0], z_send.at[i], z_recv.at[i], who).wait()
            total = z_in[0]
            for j in range(1, 8):
                total = total + z_in[j]
            z3 = rows3(total)

            def from_grad(k, _):
                r = sum3(dot(z3, g[k, chip_rows, :]))
                for i in range(CW // 128):
                    b_own[pl.ds(k * (CW // 32) + 4 * i, 4)] += r[:, i * 128 : (i + 1) * 128].reshape(4, 8, 128)
                return 0

            each = NC // 2 // PARTS
            first = (1 - core) * (NC // 2)
            for h in range(PARTS):
                lax.fori_loop(first + h * each, first + (h + 1) * each, from_grad, 0)
                core_copy(h, True)
            lax.fori_loop(core * (NC // 2), (core + 1) * (NC // 2), from_grad, 0)
            for i, who in enumerate(peer_ids):
                remote(gram_in.at[chip], gram_in.at[chip], gr_send.at[i], gr_recv.at[i], who).wait()
            total = gram_in[0]
            for j in range(1, 8):
                total = total + gram_in[j]
            gram_core[core] = total
            remote(gram_core.at[core], gram_core.at[core], pair_send.at[2], pair_recv.at[2], other).start()

            for h in range(PARTS):
                core_copy(h, False)
                b_core[h] += b_own[tiles(core, h)]
                for i, who in enumerate(ring["z"]):
                    there = fourth((z + i + 1) % 4)
                    remote(b_core.at[h, there], b_z.at[h, i], rs_send.at[0, h, i], rs_recv.at[0, h, i], who).start()
        @stage_at("e")
        def _():
            remote(gram_core.at[core], gram_core.at[core], pair_send.at[2], pair_recv.at[2], other).wait()
            packed = (gram_core[0] + gram_core[1]) * (1.0 / D_IN)
            gram_all[...] = jnp.zeros((RANK, 128), F32)
            for i in range(4):
                gram_all[i * 8 : (i + 1) * 8, 0:RANK] = packed[:, i * RANK : (i + 1) * RANK]
            sub = lax.broadcasted_iota(jnp.int32, (RANK, 128), 0)
            lane = lax.broadcasted_iota(jnp.int32, (RANK, 128), 1)
            unit = jnp.where(sub == lane, 1.0, 0.0).astype(F32)

            def eliminate(j, both):
                a, e = both
                row_a = jnp.sum(jnp.where(sub == j, a, 0.0), axis=0, keepdims=True)
                row_e = jnp.sum(jnp.where(sub == j, e, 0.0), axis=0, keepdims=True)
                col = jnp.sum(jnp.where(lane == j, a, 0.0), axis=1, keepdims=True)
                diag = jnp.sum(jnp.where(lane[0:1] == j, row_a, 0.0), axis=1, keepdims=True)
                scale = 1.0 / jnp.sqrt(diag)
                row_a, row_e = row_a * scale, row_e * scale
                factor = jnp.where(sub > j, col * scale, 0.0)
                a = jnp.where(sub == j, row_a, a - factor * row_a)
                e = jnp.where(sub == j, row_e, e - factor * row_e)
                return a, e

            linv[...] = lax.fori_loop(0, RANK, eliminate, (gram_all[...], unit))[1]
            ih, im, il = split3(linv[:, 0:RANK])
            i6[...] = jnp.concatenate([ih, ih, im, ih, il, im], axis=1)
            p_t = dot(i6[...], stack6(st[...]))
            pt_ref[...] = p_t
            ph, pm, pw = split3(p_t)
            p6[...] = jnp.concatenate([ph, ph, pm, ph, pw, pm], axis=0).T

        def landed_at(axis, stage, h, ref):
            for i, who in enumerate(ring[axis]):
                remote(ref(i), ref(i), rs_send.at[stage, h, i], rs_recv.at[stage, h, i], who).wait()

        @stage_at("f")
        def _():
            for h in range(PARTS):
                landed_at("z", 0, h, lambda i: b_z.at[h, i])
                piece_z[h] = (b_core[h, fourth(z)] + b_z[h, 0]) + (b_z[h, 1] + b_z[h, 2])
                for i, who in enumerate(ring["y"]):
                    there = pl.ds(((y + i + 1) % 4) * (PART // 16), PART // 16)
                    remote(piece_z.at[h, there], b_y.at[h, i], rs_send.at[1, h, i], rs_recv.at[1, h, i], who).start()

        @stage_at("g")
        def _():
            for h in range(PARTS):
                landed_at("y", 1, h, lambda i: b_y.at[h, i])
                own = piece_z[h, pl.ds(y * (PART // 16), PART // 16)]
                b_x[h, x] = (own + b_y[h, 0]) + (b_y[h, 1] + b_y[h, 2])
                for i, who in enumerate(ring["x"]):
                    block = b_x.at[h, x]
                    remote(block, block, rs_send.at[2, h, i], rs_recv.at[2, h, i], who).start()

        def piece(h):
            return pl.ds(core * (TILES // 2) + h * PART + z * (PART // 4) + y * (PART // 16), PART // 16)

        def pieces(h):
            return pl.ds(core * (TILES // 2) + h * PART + z * (PART // 4), PART // 4)

        def last_copy(h):
            block = q_all.at[tiles(core, h)]
            return remote(block, block, qc_send.at[h], qc_recv.at[h], other)

        @stage_at("h")
        def _():
            for h in range(PARTS):
                landed_at("x", 2, h, lambda i: b_x.at[h, x])
                q_all[piece(h)] = (b_x[h, 0] + b_x[h, 1]) + (b_x[h, 2] + b_x[h, 3])
                for i, who in enumerate(ring["y"]):
                    block = q_all.at[piece(h)]
                    remote(block, block, rs_send.at[3, h, i], rs_recv.at[3, h, i], who).start()

        @stage_at("i")
        def _():
            for h in range(PARTS):
                landed_at("y", 3, h, lambda i: q_all.at[piece(h)])
                for i, who in enumerate(ring["z"]):
                    block = q_all.at[pieces(h)]
                    remote(block, block, rs_send.at[4, h, i], rs_recv.at[4, h, i], who).start()

        @stage_at("j")
        def _():
            for h in range(PARTS):
                landed_at("z", 4, h, lambda i: q_all.at[pieces(h)])
                last_copy(h).start()

        @stage_at("k")
        def _():
            for h in range(PARTS):
                last_copy(h).wait()

        @pl.when(s >= FINISH_FROM)
        def _():
            for i in range(FINISH_EACH):
                finish((s - FINISH_FROM) * FINISH_EACH + i)

        return carry

    lax.fori_loop(0, STEPS, step, 0)

    def rest(k, carry):
        finish(k)
        return carry

    lax.fori_loop(DONE, NC, rest, 0)
    gin_out[...] = gin[...].astype(BF16)

    own_copy.wait_send()
    for flow in range(7):
        block = g.at[:, pl.ds(0, OWN)]
        remote(block, block, bulk_send.at[flow], bulk_recv.at[flow, 0], other).wait_send()
    block = g.at[:, pl.ds(0, 7 * OWN)]
    remote(block, block, core_send.at[0], core_recv.at[0], other).wait_send()


def copy_out(*refs):
    sources, targets, sem = refs[:4], refs[4:8], refs[8]
    copies = [pltpu.make_async_copy(a, b, sem.at[i]) for i, (a, b) in enumerate(zip(sources, targets))]
    for c in copies:
        c.start()
    for c in copies:
        c.wait()


def shards(acts, grad_out, weight, residue, start_q):
    vmem, dma = pltpu.VMEM, pltpu.SemaphoreType.DMA
    hbm = pl.BlockSpec(memory_space=pl.ANY)
    here = pl.BlockSpec(memory_space=pltpu.VMEM)
    flops = 4 * TOK * FEAT * D_OUT
    results = pl.pallas_call(
        kernel,
        out_shape=[
            vmem((TOK, FEAT), BF16),
            vmem((RANK, FEAT), F32),
            vmem((RANK, D_OUT), F32),
            vmem((FEAT, D_OUT), BF16),
        ],
        in_specs=[hbm] * 5,
        out_specs=[here] * 4,
        scratch_shapes=[
            vmem((NC, TOK, CW), BF16),
            vmem((FEAT, D_OUT), BF16),
            vmem((NC, FEAT, CW), F32),
            vmem((FEAT, TOK), BF16),
            vmem((TOK, FEAT), F32),
            vmem((3 * RANK, D_OUT), BF16),
            vmem((8, RANK, 128), F32),
            vmem((3 * RANK, TOK), BF16),
            vmem((RANK, FEAT), F32),
            vmem((4, RANK, FEAT), F32),
            vmem((2, RANK, FEAT), F32),
            vmem((RANK, FEAT), F32),
            vmem((3 * RANK, FEAT), BF16),
            vmem((8, RANK, 128), F32),
            vmem((8, RANK, 128), F32),
            vmem((8, 8, 128), F32),
            vmem((2, 8, 128), F32),
            vmem((RANK, 128), F32),
            vmem((RANK, 128), F32),
            vmem((RANK, 6 * RANK), BF16),
            vmem((TILES, 8, 128), F32),
            vmem((PARTS, PART, 8, 128), F32),
            vmem((PARTS, 3, PART // 4, 8, 128), F32),
            vmem((PARTS, PART // 4, 8, 128), F32),
            vmem((PARTS, 3, PART // 16, 8, 128), F32),
            vmem((PARTS, 4, PART // 16, 8, 128), F32),
            vmem((TILES, 8, 128), F32),
            vmem((RANK, CW), F32),
            vmem((6 * RANK, CW), BF16),
            vmem((FEAT, 6 * RANK), BF16),
            dma((5,)),
            dma((7,)),
            dma((7, NC)),
            dma((1,)),
            dma((NC,)),
            dma((2,)),
            dma((7,)),
            dma((7,)),
            dma((7,)),
            dma((7,)),
            dma((7,)),
            dma((7,)),
            dma((1, 3)),
            dma((1, 3)),
            dma((3,)),
            dma((3,)),
            dma((PARTS,)),
            dma((PARTS,)),
            dma((5, PARTS, 3)),
            dma((5, PARTS, 3)),
            dma((PARTS,)),
            dma((PARTS,)),
        ],
        compiler_params=pltpu.CompilerParams(
            collective_id=1, has_side_effects=True, vmem_limit_bytes=46 * 2**20
        ),
        cost_estimate=pl.CostEstimate(flops=flops, bytes_accessed=24 * 2**20, transcendentals=0),
        name="gather_and_compress",
    )(*(pltpu.with_memory_space_constraint(a, pltpu.HBM) for a in (acts, grad_out, weight, residue[0], start_q.T)))
    grad_in, p_t, q_t, new = pl.pallas_call(
        copy_out,
        out_shape=[jax.ShapeDtypeStruct(r.shape, r.dtype) for r in results],
        in_specs=[here] * 4,
        out_specs=[hbm] * 4,
        scratch_shapes=[dma((4,))],
        compiler_params=pltpu.CompilerParams(vmem_limit_bytes=4 * 2**20),
        name="copy_out",
    )(*(pltpu.with_memory_space_constraint(r, pltpu.VMEM) for r in results))
    return grad_in, p_t.T, q_t.T, new[None]


def solution(mesh):
    in_specs = (
        P("dp", "tensor"),
        P(("dp", "tensor"), None),
        P("tensor", None),
        P("dp", "tensor", None),
        P(),
    )
    out_specs = (P("dp", "tensor"), P("tensor", None), P(), P("dp", "tensor", None))
    return jax.shard_map(shards, mesh=mesh, in_specs=in_specs, out_specs=out_specs, check_vma=False)
```

time: 101 us -> 82.7 us (0.82)
  local copies, waits for them, and re-layouts: 12 us -> 0 us
  Pallas kernels: 88.3 us -> 81.9 us
    unnamed x4 -> x0, local copies, waits for them, and re-layouts: 12 us -> none
    pallas_call x1 -> x2, Pallas kernels: 88.3 us -> 81.9 us  [the longest x1 78.5 us: shards(): pl.pallas_call(kernel, out_shape=[vmem((TOK, FEAT), BF16), vmem((RANK, FE...]
where the time goes in v2:
time: 82.7 us; the launch traced here: 82.6 us
  Pallas kernels  81.9 us (99%)
    pallas_call x1, Pallas kernels, shards(): pl.pallas_call(kernel, out_shape=[vmem((TOK, FEAT), BF16), vmem((RANK, FE...  78.5 us
    pallas_call x1, Pallas kernels, shards(): pl.pallas_call(copy_out, out_shape=[jax.ShapeDtypeStruct(r.shape, r.dtype...  3.37 us

profile of v2, /device:TPU:1, one launch (start us, length us, event | category | flops | bytes accessed | tf_op | source)
XLA Modules:
  0.0 82.6 jit_solution(14782904488412370874)
XLA Ops:
  0.6 78.5 %gather_and_compress.1 = (bf16[1024,512]{1,0:T(8,128)(2,1)S(1)}, f32[32,512]{1,0:T(8,128)S(1)}, f32[32,6144]{1,0:T(8,128)S(1)}, bf16[512,6144]{1,0:T(8,128)(2,1)S(1)}) custom-call(bf16[1024,512]{1,0:T(8,128)(2,1)} %acts_hbm.1, bf16[64,6144]{1,0:T(8,128)(2,1)} %grad_hbm.1, bf16[512,6144]{1,0:T(8,128)(2,1)} %weight_hbm.1, bf16[512,6144]{1,0:T(8,128)(2,1)} %bitcast.5, ...), custom_call_target="tpu_custom_call" | custom-call | flops 12884901888 | bytes 25165824 | tf_op jit(solution)/shard_map/gather_and_compress/pallas_call | solution.py:458
  79.2 3.4 %copy_out.1 = (bf16[1024,512]{1,0:T(8,128)(2,1)}, f32[32,512]{1,0:T(8,128)}, f32[32,6144]{1,0:T(8,128)}, bf16[512,6144]{1,0:T(8,128)(2,1)}) custom-call(bf16[1024,512]{1,0:T(8,128)(2,1)S(1)} %get-tuple-element.12.refs_0_, f32[32,512]{1,0:T(8,128)S(1)} %get-tuple-element.13.refs_1_, f32[32,6144]{1,0:T(8,128)S(1)} %get-tuple-element.14.refs_2_, ...), custom_call_target="tpu_custom_call" | custom-call | tf_op jit(solution)/shard_map/copy_out/pallas_call | solution.py:528

commit v3 on v2

--- a/solution.py
+++ b/solution.py
@@ -16,14 +16,12 @@
 NC = D_OUT // CW
 NT = (((1,), (1,)), ((), ()))
 
-STAGE_AT = dict(a=1, b=3, c=4, d=5, e=8, f=7, g=8, h=9, i=10, j=11, k=12)
+STAGE_AT = dict(a=1, b=3, c=5, d=7, e=9, f=9, g=10, h=11, i=12, j=13, k=14)
 PARTS = 3
 TILES = D_OUT // 128 * RANK // 8
 PART = TILES // 2 // PARTS
 STEPS = NC + 7
 EARLY = 3
-FINISH_FROM, FINISH_EACH = 13, 2
-DONE = (STEPS - FINISH_FROM) * FINISH_EACH
 
 
 def place():
@@ -58,21 +56,26 @@
     return v[:n] + (v[n : 2 * n] + v[2 * n :])
 
 
+def stack6(v):
+    h, m, low = split3(v)
+    return jnp.concatenate([h, m, h, low, h, m], axis=0)
+
+
 def dot(a, b, dims=(((1,), (0,)), ((), ()))):
     return lax.dot_general(a, b, dims, preferred_element_type=F32)
 
 
 def kernel(
     acts_hbm, grad_hbm, weight_hbm, residue_hbm, qt_hbm,
-    gin_out, pt_ref, qt_out_ref, new_ref,
-    g, weight, merged, acts_t, gin,
-    qt3, gq, gq3, part, sk_z, sk_y, st, st3, z_out, z_in, gram_in, gram_core, gram_all, linv, i6,
-    b_own, b_core, b_z, piece_z, b_y, b_x, q_all, b_t, q6, p6,
+    gin_out, pt_ref, q_out, merged, i6, p6,
+    g, pair_g, weight, residue, acts_t, gin, qt,
+    qt3, gq_half, gq, gq3, part, ska_z, ska_y, skb_y, skb_z, st, st3, z_out, z_in, gram_in, gram_core, gram_all, linv,
+    b_own, b_core, b_z, piece_z, b_y, b_x, q_all,
     load_sem, bulk_send, bulk_recv, core_send, core_recv, own_sem,
     gq_send, gq_recv, z_send, z_recv, gr_send, gr_recv, ring_send, ring_recv, pair_send, pair_recv,
     bc_send, bc_recv, rs_send, rs_recv, qc_send, qc_recv,
 ):
-    acts, qt, residue = gin_out, qt_out_ref, new_ref
+    acts = gin_out
     at = place()
     x, y_hi, y_lo, z, core = at["x"], at["y_hi"], at["y_lo"], at["z"], at["core"]
     y = y_hi * 2 + y_lo
@@ -87,20 +90,18 @@
         "z": [device(at, z=(z + i) % 4) for i in (1, 2, 3)],
     }
 
-    def own_rows(dx, dy):
-        t = ((x + dx + 4) % 4) * 4 + ((y_hi + dy) % 2) * 2 + core
-        return pl.ds(pl.multiple_of(t * OWN, OWN), OWN)
-
-    mine = own_rows(0, 0)
-    chip_rows = pl.ds(pl.multiple_of(chip * 2 * OWN, 2 * OWN), 2 * OWN)
+    def chip_at(dx, dy):
+        return ((x + dx + 4) % 4) * 2 + (y_hi + dy) % 2
+
+    beyond, over = chip_at(2, 0), chip_at(0, 1)
 
     def chunk(k):
         return pl.ds(pl.multiple_of(k * CW, CW), CW)
 
     for k in range(NC):
-        pltpu.make_async_copy(
-            grad_hbm.at[:, pl.ds(k * CW, CW)], g.at[k, mine], load_sem.at[0]
-        ).start()
+        own = grad_hbm.at[:, pl.ds(k * CW, CW)]
+        pltpu.make_async_copy(own, pair_g.at[k, core], load_sem.at[0]).start()
+        pltpu.make_async_copy(own, g.at[k, chip, core], load_sem.at[5]).start()
     load_q = pltpu.make_async_copy(qt_hbm, qt, load_sem.at[1])
     load_res = pltpu.make_async_copy(residue_hbm, residue, load_sem.at[2])
     load_acts = pltpu.make_async_copy(acts_hbm, acts, load_sem.at[3])
@@ -116,7 +117,14 @@
         pl.semaphore_signal(barrier, inc=1, device_id=who, device_id_type=MESH)
     load_q.wait()
     qt3[...] = rows3(qt[...])
-    pltpu.make_async_copy(g.at[:, mine], g.at[:, mine], load_sem.at[0]).wait()
+    pltpu.make_async_copy(pair_g.at[:, core], pair_g.at[:, core], load_sem.at[0]).wait()
+    pltpu.make_async_copy(g.at[:, chip, core], g.at[:, chip, core], load_sem.at[5]).wait()
+    total = jnp.zeros((3 * RANK, 2 * OWN), F32)
+    for k in range(NC):
+        twice = jnp.concatenate([pair_g[k, core], pair_g[k, core]], axis=0)
+        total += dot(qt3[:, k * CW : (k + 1) * CW], twice, NT)
+    lane = lax.broadcasted_iota(jnp.int32, (RANK, 2 * OWN), 1)
+    gq_half[core] = jnp.where(lane // OWN == core, sum3(total), 0.0)
     pl.semaphore_wait(barrier, len(greet))
 
     def remote(src, dst, send, recv, who):
@@ -124,39 +132,28 @@
             src_ref=src, dst_ref=dst, send_sem=send, recv_sem=recv, device_id=who, device_id_type=MESH
         )
 
-    def bulk(flow, k, rows, who):
-        block = g.at[k, rows]
+    def bulk(flow, k, source, who):
+        block = g.at[k, source, core]
         return remote(block, block, bulk_send.at[flow], bulk_recv.at[flow, k], who)
 
     def arrived(flow, k):
-        bulk(flow, k, mine, other).wait_recv()
-
-    def to_core(k, rows):
-        block = g.at[k, rows]
-        remote(block, block, core_send.at[0], core_recv.at[k], other).start()
+        bulk(flow, k, chip, other).wait_recv()
+
+    def to_core(k):
+        plane = g.at[k, :, core]
+        return remote(plane, plane, core_send.at[0], core_recv.at[k], other)
 
     right, left, across = ring["x"][0], ring["x"][2], device(at, y_hi=1 - y_hi)
 
-    own_copy = remote(g.at[:, mine], g.at[:, mine], own_sem.at[0], own_sem.at[1], other)
+    own_copy = remote(pair_g.at[:, core], pair_g.at[:, core], own_sem.at[0], own_sem.at[1], other)
+    half_copy = remote(gq_half.at[core], gq_half.at[core], own_sem.at[2], own_sem.at[3], other)
+    half_copy.start()
     own_copy.start()
 
-    def stack6(v):
-        h, m, low = split3(v)
-        return jnp.concatenate([h, m, h, low, h, m], axis=0)
-
-    def finish(k):
-        for i in range(CW // 128):
-            block = q_all[pl.ds(k * (CW // 32) + 4 * i, 4)]
-            b_t[:, i * 128 : (i + 1) * 128] = block.reshape(RANK, 128)
-        q_t = dot(i6[...], stack6(b_t[...])) * (1.0 / (REPLICAS * math.sqrt(D_IN)))
-        qt_out_ref[:, chunk(k)] = q_t
-        q6[...] = stack6(q_t * (1.0 / math.sqrt(D_IN)))
-        new_ref[:, chunk(k)] = (merged[k] - dot(p6[...], q6[...])).astype(BF16)
-
     def send_own(k):
-        bulk(0, k, mine, right).start()
-        bulk(1, k, mine, left).start()
-        bulk(2, k, mine, across).start()
+        bulk(0, k, chip, right).start()
+        bulk(1, k, chip, left).start()
+        bulk(2, k, chip, across).start()
 
     def step(s, carry):
         @pl.when((s >= EARLY) & (s < NC))
@@ -166,11 +163,8 @@
         @pl.when(s == 0)
         def _():
             send_own(0)
-            own_copy.wait_recv()
-            total = jnp.zeros((3 * RANK, 2 * OWN), F32)
-            for k in range(NC):
-                total += dot(qt3[:, k * CW : (k + 1) * CW], g[k, chip_rows, :], NT)
-            gq[chip] = sum3(total)
+            half_copy.wait()
+            gq[chip] = gq_half[0] + gq_half[1]
             for i, who in enumerate(peer_ids):
                 remote(gq.at[chip], gq.at[chip], gq_send.at[i], gq_recv.at[i], who).start()
             for k in range(1, EARLY):
@@ -192,30 +186,24 @@
             arrived(1, k)
             odd = k % 2
             ahead = device(at, x=(x + 1 + 2 * odd) % 4)
-            bulk(3, k, own_rows(2 * odd - 1, 0), ahead).start()
+            bulk(3, k, chip_at(2 * odd - 1, 0), ahead).start()
             arrived(2, k)
-            bulk(4, k, own_rows(0, 1), right).start()
-            bulk(5, k, own_rows(0, 1), left).start()
-            to_core(k, own_rows(-1, 0))
-            to_core(k, own_rows(1, 0))
-            to_core(k, own_rows(0, 1))
+            bulk(4, k, over, right).start()
+            bulk(5, k, over, left).start()
 
         @pl.when((s >= 4) & (s < NC + 4))
         def _():
             k = s - 4
             arrived(3, k)
-            bulk(6, k, own_rows(2, 0), across).start()
-            to_core(k, own_rows(2, 0))
+            bulk(6, k, beyond, across).start()
             arrived(4, k)
-            to_core(k, own_rows(-1, 1))
             arrived(5, k)
-            to_core(k, own_rows(1, 1))
 
         @pl.when((s >= 6) & (s < NC + 6))
         def _():
             k = s - 6
             arrived(6, k)
-            to_core(k, own_rows(2, 1))
+            to_core(k).start()
 
         @pl.when(s == 4)
         def _():
@@ -224,13 +212,23 @@
         @pl.when(s >= 7)
         def _():
             k = s - 7
-            landed = g.at[k, pl.ds(0, 7 * OWN)]
-            remote(landed, landed, core_send.at[0], core_recv.at[k], other).wait_recv()
-            merged[k] = dot(acts_t[...], g[k]) + residue[:, chunk(k)].astype(F32)
-            gin[...] += dot(g[k], weight[:, chunk(k)], NT)
+            to_core(k).wait_recv()
+            rows = g[k].reshape(TOK, CW)
+            merged[k] = dot(acts_t[...], rows) + residue[:, chunk(k)].astype(F32)
+            gin[...] += dot(rows, weight[:, chunk(k)], NT)
 
         def stage_at(name):
             return pl.when(s == STAGE_AT[name])
+
+        def z_copies(ref, n):
+            return [
+                remote(ref.at[z], ref.at[z], ring_send.at[n, i], ring_recv.at[n, i], who)
+                for i, who in enumerate(ring["z"])
+            ]
+
+        def y_copy(ref, n):
+            near = device(at, y_lo=1 - y_lo)
+            return remote(ref.at[y_lo], ref.at[y_lo], pair_send.at[n], pair_recv.at[n], near)
 
         @stage_at("a")
         def _():
@@ -238,21 +236,32 @@
                 remote(gq.at[chip], gq.at[chip], gq_send.at[i], gq_recv.at[i], who).wait()
             for j in range(8):
                 gq3[:, j * 128 : (j + 1) * 128] = rows3(gq[j])
-            sk_z[z] = part[...] + sum3(dot(gq3[...], acts[...]))
-            for i, who in enumerate(ring["z"]):
-                remote(sk_z.at[z], sk_z.at[z], ring_send.at[0, i], ring_recv.at[0, i], who).start()
+            sketch = part[...] + sum3(dot(gq3[...], acts[...]))
+            ska_z[z] = sketch[:, : FEAT // 2]
+            skb_y[y_lo] = sketch[:, FEAT // 2 :]
+            y_copy(skb_y, 0).start()
+            for c in z_copies(ska_z, 0):
+                c.start()
 
         @stage_at("b")
         def _():
-            for i, who in enumerate(ring["z"]):
-                remote(sk_z.at[z], sk_z.at[z], ring_send.at[0, i], ring_recv.at[0, i], who).wait()
-            sk_y[y_lo] = (sk_z[0] + sk_z[1]) + (sk_z[2] + sk_z[3])
-            remote(sk_y.at[y_lo], sk_y.at[y_lo], pair_send.at[0], pair_recv.at[0], device(at, y_lo=1 - y_lo)).start()
+            y_copy(skb_y, 0).wait()
+            skb_z[z] = skb_y[0] + skb_y[1]
+            for c in z_copies(skb_z, 1):
+                c.start()
+            for c in z_copies(ska_z, 0):
+                c.wait()
+            ska_y[y_lo] = (ska_z[0] + ska_z[1]) + (ska_z[2] + ska_z[3])
+            y_copy(ska_y, 1).start()
 
         @stage_at("c")
         def _():
-            remote(sk_y.at[y_lo], sk_y.at[y_lo], pair_send.at[0], pair_recv.at[0], device(at, y_lo=1 - y_lo)).wait()
-            sketch = (sk_y[0] + sk_y[1]) * (1.0 / REPLICAS)
+            y_copy(ska_y, 1).wait()
+            for c in z_copies(skb_z, 1):
+                c.wait()
+            low = ska_y[0] + ska_y[1]
+            high = (skb_z[0] + skb_z[1]) + (skb_z[2] + skb_z[3])
+            sketch = jnp.concatenate([low, high], axis=1) * (1.0 / REPLICAS)
             st[...] = sketch
             st3[...] = rows3(sketch)
             zt = sum3(dot(st3[...], acts_t[...]))
@@ -297,9 +306,10 @@
             for j in range(1, 8):
                 total = total + z_in[j]
             z3 = rows3(total)
+            own_copy.wait_recv()
 
             def from_grad(k, _):
-                r = sum3(dot(z3, g[k, chip_rows, :]))
+                r = sum3(dot(z3, pair_g[k].reshape(2 * OWN, CW)))
                 for i in range(CW // 128):
                     b_own[pl.ds(k * (CW // 32) + 4 * i, 4)] += r[:, i * 128 : (i + 1) * 128].reshape(4, 8, 128)
                 return 0
@@ -417,37 +427,48 @@
             for h in range(PARTS):
                 last_copy(h).wait()
 
-        @pl.when(s >= FINISH_FROM)
-        def _():
-            for i in range(FINISH_EACH):
-                finish((s - FINISH_FROM) * FINISH_EACH + i)
-
         return carry
 
     lax.fori_loop(0, STEPS, step, 0)
 
-    def rest(k, carry):
-        finish(k)
-        return carry
-
-    lax.fori_loop(DONE, NC, rest, 0)
+    q_out[...] = q_all[...]
     gin_out[...] = gin[...].astype(BF16)
 
     own_copy.wait_send()
     for flow in range(7):
-        block = g.at[:, pl.ds(0, OWN)]
+        block = g.at[:, 0, 0]
         remote(block, block, bulk_send.at[flow], bulk_recv.at[flow, 0], other).wait_send()
-    block = g.at[:, pl.ds(0, 7 * OWN)]
+    block = g.at[:, :, core]
     remote(block, block, core_send.at[0], core_recv.at[0], other).wait_send()
 
 
-def copy_out(*refs):
-    sources, targets, sem = refs[:4], refs[4:8], refs[8]
-    copies = [pltpu.make_async_copy(a, b, sem.at[i]) for i, (a, b) in enumerate(zip(sources, targets))]
-    for c in copies:
-        c.start()
-    for c in copies:
-        c.wait()
+def finish(
+    gin, p_t, q_all, merged, i6, p6, gin_hbm, pt_hbm, qt_hbm, new_hbm, new, q_t, b_t, q6, sem
+):
+    store_gin = pltpu.make_async_copy(gin, gin_hbm, sem.at[0])
+    store_p = pltpu.make_async_copy(p_t, pt_hbm, sem.at[1])
+    store_gin.start()
+    store_p.start()
+
+    def body(k, carry):
+        columns = pl.ds(pl.multiple_of(k * CW, CW), CW)
+        for i in range(CW // 128):
+            block = q_all[pl.ds(k * (CW // 32) + 4 * i, 4)]
+            b_t[:, i * 128 : (i + 1) * 128] = block.reshape(RANK, 128)
+        q = dot(i6[...], stack6(b_t[...])) * (1.0 / (REPLICAS * math.sqrt(D_IN)))
+        q_t[:, columns] = q
+        q6[...] = stack6(q * (1.0 / math.sqrt(D_IN)))
+        new[k] = (merged[k] - dot(p6[...], q6[...])).astype(BF16)
+        pltpu.make_async_copy(new.at[k], new_hbm.at[:, columns], sem.at[2]).start()
+        return carry
+
+    lax.fori_loop(0, NC, body, 0)
+    store_q = pltpu.make_async_copy(q_t, qt_hbm, sem.at[3])
+    store_q.start()
+    pltpu.make_async_copy(new, new, sem.at[2]).wait()
+    store_gin.wait()
+    store_p.wait()
+    store_q.wait()
 
 
 def shards(acts, grad_out, weight, residue, start_q):
@@ -460,23 +481,30 @@
         out_shape=[
             vmem((TOK, FEAT), BF16),
             vmem((RANK, FEAT), F32),
-            vmem((RANK, D_OUT), F32),
-            vmem((FEAT, D_OUT), BF16),
+            vmem((TILES, 8, 128), F32),
+            vmem((NC, FEAT, CW), F32),
+            vmem((RANK, 6 * RANK), BF16),
+            vmem((FEAT, 6 * RANK), BF16),
         ],
         in_specs=[hbm] * 5,
-        out_specs=[here] * 4,
+        out_specs=[here] * 6,
         scratch_shapes=[
-            vmem((NC, TOK, CW), BF16),
+            vmem((NC, TOK // OWN // 2, 2, OWN, CW), BF16),
+            vmem((NC, 2, OWN, CW), BF16),
             vmem((FEAT, D_OUT), BF16),
-            vmem((NC, FEAT, CW), F32),
+            vmem((FEAT, D_OUT), BF16),
             vmem((FEAT, TOK), BF16),
             vmem((TOK, FEAT), F32),
+            vmem((RANK, D_OUT), F32),
             vmem((3 * RANK, D_OUT), BF16),
+            vmem((2, RANK, 128), F32),
             vmem((8, RANK, 128), F32),
             vmem((3 * RANK, TOK), BF16),
             vmem((RANK, FEAT), F32),
-            vmem((4, RANK, FEAT), F32),
-            vmem((2, RANK, FEAT), F32),
+            vmem((4, RANK, FEAT // 2), F32),
+            vmem((2, RANK, FEAT // 2), F32),
+            vmem((2, RANK, FEAT // 2), F32),
+            vmem((4, RANK, FEAT // 2), F32),
             vmem((RANK, FEAT), F32),
             vmem((3 * RANK, FEAT), BF16),
             vmem((8, RANK, 128), F32),
@@ -485,7 +513,6 @@
             vmem((2, 8, 128), F32),
             vmem((RANK, 128), F32),
             vmem((RANK, 128), F32),
-            vmem((RANK, 6 * RANK), BF16),
             vmem((TILES, 8, 128), F32),
             vmem((PARTS, PART, 8, 128), F32),
             vmem((PARTS, 3, PART // 4, 8, 128), F32),
@@ -493,23 +520,20 @@
             vmem((PARTS, 3, PART // 16, 8, 128), F32),
             vmem((PARTS, 4, PART // 16, 8, 128), F32),
             vmem((TILES, 8, 128), F32),
-            vmem((RANK, CW), F32),
-            vmem((6 * RANK, CW), BF16),
-            vmem((FEAT, 6 * RANK), BF16),
-            dma((5,)),
+            dma((6,)),
             dma((7,)),
             dma((7, NC)),
             dma((1,)),
             dma((NC,)),
-            dma((2,)),
-            dma((7,)),
-            dma((7,)),
-            dma((7,)),
-            dma((7,)),
-            dma((7,)),
-            dma((7,)),
-            dma((1, 3)),
-            dma((1, 3)),
+            dma((4,)),
+            dma((7,)),
+            dma((7,)),
+            dma((7,)),
+            dma((7,)),
+            dma((7,)),
+            dma((7,)),
+            dma((2, 3)),
+            dma((2, 3)),
             dma((3,)),
             dma((3,)),
             dma((PARTS,)),
@@ -520,19 +544,30 @@
             dma((PARTS,)),
         ],
         compiler_params=pltpu.CompilerParams(
-            collective_id=1, has_side_effects=True, vmem_limit_bytes=46 * 2**20
+            collective_id=1, has_side_effects=True, vmem_limit_bytes=40 * 2**20
         ),
         cost_estimate=pl.CostEstimate(flops=flops, bytes_accessed=24 * 2**20, transcendentals=0),
         name="gather_and_compress",
     )(*(pltpu.with_memory_space_constraint(a, pltpu.HBM) for a in (acts, grad_out, weight, residue[0], start_q.T)))
     grad_in, p_t, q_t, new = pl.pallas_call(
-        copy_out,
-        out_shape=[jax.ShapeDtypeStruct(r.shape, r.dtype) for r in results],
-        in_specs=[here] * 4,
+        finish,
+        out_shape=[
+            jax.ShapeDtypeStruct((TOK, FEAT), BF16),
+            jax.ShapeDtypeStruct((RANK, FEAT), F32),
+            jax.ShapeDtypeStruct((RANK, D_OUT), F32),
+            jax.ShapeDtypeStruct((FEAT, D_OUT), BF16),
+        ],
+        in_specs=[here] * 6,
         out_specs=[hbm] * 4,
-        scratch_shapes=[dma((4,))],
-        compiler_params=pltpu.CompilerParams(vmem_limit_bytes=4 * 2**20),
-        name="copy_out",
+        scratch_shapes=[
+            vmem((NC, FEAT, CW), BF16),
+            vmem((RANK, D_OUT), F32),
+            vmem((RANK, CW), F32),
+            vmem((6 * RANK, CW), BF16),
+            dma((4,)),
+        ],
+        compiler_params=pltpu.CompilerParams(vmem_limit_bytes=14 * 2**20),
+        name="finish",
     )(*(pltpu.with_memory_space_constraint(r, pltpu.VMEM) for r in results))
     return grad_in, p_t.T, q_t.T, new[None]
 

time: 82.7 us -> 80.1 us (0.969)
  Pallas kernels: 81.9 us -> 79.3 us
    pallas_call x1, Pallas kernels: 78.5 us -> 73 us  [shards(): pl.pallas_call(kernel, out_shape=[vmem((TOK, FEAT), BF16), vmem((RANK, FE...]
    pallas_call x1, Pallas kernels: 3.37 us -> 6.34 us  [shards(): pl.pallas_call(finish, out_shape=[jax.ShapeDtypeStruct((TOK, FEAT), BF16)...]
where the time goes in v3:
time: 80.1 us; the launch traced here: 80 us
  Pallas kernels  79.3 us (99%)
    pallas_call x1, Pallas kernels, shards(): pl.pallas_call(kernel, out_shape=[vmem((TOK, FEAT), BF16), vmem((RANK, FE...  73 us
    pallas_call x1, Pallas kernels, shards(): pl.pallas_call(finish, out_shape=[jax.ShapeDtypeStruct((TOK, FEAT), BF16)...  6.34 us

profile of v3, /device:TPU:1, one launch (start us, length us, event | category | flops | bytes accessed | tf_op | source)
XLA Modules:
  0.0 80.0 jit_solution(3425523725640775869)
XLA Ops:
  0.6 73.0 %gather_and_compress.1 = (bf16[1024,512]{1,0:T(8,128)(2,1)S(1)}, f32[32,512]{1,0:T(8,128)S(1)}, f32[192,8,128]{2,1,0:T(8,128)S(1)}, f32[12,512,512]{2,1,0:T(8,12...) custom-call(bf16[1024,512]{1,0:T(8,128)(2,1)} %acts_hbm.1, bf16[64,6144]{1,0:T(8,128)(2,1)} %grad_hbm.1, ...), custom_call_target="tpu_custom_call" | custom-call | flops 12884901888 | bytes 25165824 | tf_op jit(solution)/shard_map/gather_and_compress/pallas_call | solution.py:479
  73.6 6.3 %finish.1 = (bf16[1024,512]{1,0:T(8,128)(2,1)}, f32[32,512]{1,0:T(8,128)}, f32[32,6144]{1,0:T(8,128)}, bf16[512,6144]{1,0:T(8,128)(2,1)}) custom-call(bf16[1024,512]{1,0:T(8,128)(2,1)S(1)} %get-tuple-element.14.gin, f32[32,512]{1,0:T(8,128)S(1)} %get-tuple-element.15.p_t, f32[192,8,128]{2,1,0:T(8,128)S(1)} %get-tuple-element.16.q_all, ...), custom_call_target="tpu_custom_call" | custom-call | tf_op jit(solution)/shard_map/finish/pallas_call | solution.py:552

commit v4 on v3

--- a/solution.py
+++ b/solution.py
@@ -21,6 +21,7 @@
 TILES = D_OUT // 128 * RANK // 8
 PART = TILES // 2 // PARTS
 STEPS = NC + 7
+WIDE = 3072
 EARLY = 3
 
 
@@ -450,21 +451,26 @@
     store_gin.start()
     store_p.start()
 
-    def body(k, carry):
-        columns = pl.ds(pl.multiple_of(k * CW, CW), CW)
-        for i in range(CW // 128):
-            block = q_all[pl.ds(k * (CW // 32) + 4 * i, 4)]
+    def right(j, carry):
+        columns = pl.ds(pl.multiple_of(j * WIDE, WIDE), WIDE)
+        for i in range(WIDE // 128):
+            block = q_all[pl.ds(j * (WIDE // 32) + 4 * i, 4)]
             b_t[:, i * 128 : (i + 1) * 128] = block.reshape(RANK, 128)
         q = dot(i6[...], stack6(b_t[...])) * (1.0 / (REPLICAS * math.sqrt(D_IN)))
         q_t[:, columns] = q
-        q6[...] = stack6(q * (1.0 / math.sqrt(D_IN)))
-        new[k] = (merged[k] - dot(p6[...], q6[...])).astype(BF16)
+        q6[:, columns] = stack6(q * (1.0 / math.sqrt(D_IN)))
+        return carry
+
+    def body(k, carry):
+        columns = pl.ds(pl.multiple_of(k * CW, CW), CW)
+        new[k] = (merged[k] - dot(p6[...], q6[:, columns])).astype(BF16)
         pltpu.make_async_copy(new.at[k], new_hbm.at[:, columns], sem.at[2]).start()
         return carry
 
-    lax.fori_loop(0, NC, body, 0)
+    lax.fori_loop(0, D_OUT // WIDE, right, 0)
     store_q = pltpu.make_async_copy(q_t, qt_hbm, sem.at[3])
     store_q.start()
+    lax.fori_loop(0, NC, body, 0, unroll=3)
     pltpu.make_async_copy(new, new, sem.at[2]).wait()
     store_gin.wait()
     store_p.wait()
@@ -562,8 +568,8 @@
         scratch_shapes=[
             vmem((NC, FEAT, CW), BF16),
             vmem((RANK, D_OUT), F32),
-            vmem((RANK, CW), F32),
-            vmem((6 * RANK, CW), BF16),
+            vmem((RANK, WIDE), F32),
+            vmem((6 * RANK, D_OUT), BF16),
             dma((4,)),
         ],
         compiler_params=pltpu.CompilerParams(vmem_limit_bytes=14 * 2**20),

time: 80.1 us -> 77.6 us (0.969)
  Pallas kernels: 79.3 us -> 76.9 us
    pallas_call x1, Pallas kernels: 6.34 us -> 3.88 us  [shards(): pl.pallas_call(finish, out_shape=[jax.ShapeDtypeStruct((TOK, FEAT), BF16)...]
where the time goes in v4:
time: 77.6 us; the launch traced here: 77.5 us
  Pallas kernels  76.9 us (99%)
    pallas_call x1, Pallas kernels, shards(): pl.pallas_call(kernel, out_shape=[vmem((TOK, FEAT), BF16), vmem((RANK, FE...  73 us
    pallas_call x1, Pallas kernels, shards(): pl.pallas_call(finish, out_shape=[jax.ShapeDtypeStruct((TOK, FEAT), BF16)...  3.88 us

profile of v4, /device:TPU:1, one launch (start us, length us, event | category | flops | bytes accessed | tf_op | source)
XLA Modules:
  0.0 77.5 jit_solution(2502275682008972203)
XLA Ops:
  0.6 73.0 %gather_and_compress.1 = (bf16[1024,512]{1,0:T(8,128)(2,1)S(1)}, f32[32,512]{1,0:T(8,128)S(1)}, f32[192,8,128]{2,1,0:T(8,128)S(1)}, f32[12,512,512]{2,1,0:T(8,12...) custom-call(bf16[1024,512]{1,0:T(8,128)(2,1)} %acts_hbm.1, bf16[64,6144]{1,0:T(8,128)(2,1)} %grad_hbm.1, ...), custom_call_target="tpu_custom_call" | custom-call | flops 12884901888 | bytes 25165824 | tf_op jit(solution)/shard_map/gather_and_compress/pallas_call | solution.py:485
  73.6 3.9 %finish.1 = (bf16[1024,512]{1,0:T(8,128)(2,1)}, f32[32,512]{1,0:T(8,128)}, f32[32,6144]{1,0:T(8,128)}, bf16[512,6144]{1,0:T(8,128)(2,1)}) custom-call(bf16[1024,512]{1,0:T(8,128)(2,1)S(1)} %get-tuple-element.14.gin, f32[32,512]{1,0:T(8,128)S(1)} %get-tuple-element.15.p_t, f32[192,8,128]{2,1,0:T(8,128)S(1)} %get-tuple-element.16.q_all, ...), custom_call_target="tpu_custom_call" | custom-call | tf_op jit(solution)/shard_map/finish/pallas_call | solution.py:558

commit v5 on v4

--- a/solution.py
+++ b/solution.py
@@ -33,6 +33,10 @@
 def device(at, **moved):
     q = {**at, **moved}
     return {"dp": q["y_lo"] * 4 + q["z"], "tensor": q["x"] * 4 + q["y_hi"] * 2 + q["core"]}
+
+
+def far_first(ring):
+    return [(i, ring[i]) for i in (1, 0, 2)]
 
 
 def along_y(at, by):
@@ -83,7 +87,7 @@
     me = x * 4 + y_hi * 2 + core
     chip = x * 2 + y_hi
     other = device(at, core=1 - core)
-    peers = [(dx, dy) for dx in range(4) for dy in range(2) if (dx, dy) != (0, 0)]
+    peers = [(2, 1), (1, 1), (3, 1), (2, 0), (0, 1), (1, 0), (3, 0)]
     peer_ids = [device(at, x=(x + dx) % 4, y_hi=(y_hi + dy) % 2) for dx, dy in peers]
     ring = {
         "x": [device(at, x=(x + i) % 4) for i in (1, 2, 3)],
@@ -224,7 +228,7 @@
         def z_copies(ref, n):
             return [
                 remote(ref.at[z], ref.at[z], ring_send.at[n, i], ring_recv.at[n, i], who)
-                for i, who in enumerate(ring["z"])
+                for i, who in far_first(ring["z"])
             ]
 
         def y_copy(ref, n):
@@ -332,7 +336,7 @@
             for h in range(PARTS):
                 core_copy(h, False)
                 b_core[h] += b_own[tiles(core, h)]
-                for i, who in enumerate(ring["z"]):
+                for i, who in far_first(ring["z"]):
                     there = fourth((z + i + 1) % 4)
                     remote(b_core.at[h, there], b_z.at[h, i], rs_send.at[0, h, i], rs_recv.at[0, h, i], who).start()
         @stage_at("e")
@@ -368,7 +372,7 @@
             p6[...] = jnp.concatenate([ph, ph, pm, ph, pw, pm], axis=0).T
 
         def landed_at(axis, stage, h, ref):
-            for i, who in enumerate(ring[axis]):
+            for i, who in far_first(ring[axis]):
                 remote(ref(i), ref(i), rs_send.at[stage, h, i], rs_recv.at[stage, h, i], who).wait()
 
         @stage_at("f")
@@ -376,7 +380,7 @@
             for h in range(PARTS):
                 landed_at("z", 0, h, lambda i: b_z.at[h, i])
                 piece_z[h] = (b_core[h, fourth(z)] + b_z[h, 0]) + (b_z[h, 1] + b_z[h, 2])
-                for i, who in enumerate(ring["y"]):
+                for i, who in far_first(ring["y"]):
                     there = pl.ds(((y + i + 1) % 4) * (PART // 16), PART // 16)
                     remote(piece_z.at[h, there], b_y.at[h, i], rs_send.at[1, h, i], rs_recv.at[1, h, i], who).start()
 
@@ -386,7 +390,7 @@
                 landed_at("y", 1, h, lambda i: b_y.at[h, i])
                 own = piece_z[h, pl.ds(y * (PART // 16), PART // 16)]
                 b_x[h, x] = (own + b_y[h, 0]) + (b_y[h, 1] + b_y[h, 2])
-                for i, who in enumerate(ring["x"]):
+                for i, who in far_first(ring["x"]):
                     block = b_x.at[h, x]
                     remote(block, block, rs_send.at[2, h, i], rs_recv.at[2, h, i], who).start()
 
@@ -405,7 +409,7 @@
             for h in range(PARTS):
                 landed_at("x", 2, h, lambda i: b_x.at[h, x])
                 q_all[piece(h)] = (b_x[h, 0] + b_x[h, 1]) + (b_x[h, 2] + b_x[h, 3])
-                for i, who in enumerate(ring["y"]):
+                for i, who in far_first(ring["y"]):
                     block = q_all.at[piece(h)]
                     remote(block, block, rs_send.at[3, h, i], rs_recv.at[3, h, i], who).start()
 
@@ -413,7 +417,7 @@
         def _():
             for h in range(PARTS):
                 landed_at("y", 3, h, lambda i: q_all.at[piece(h)])
-                for i, who in enumerate(ring["z"]):
+                for i, who in far_first(ring["z"]):
                     block = q_all.at[pieces(h)]
                     remote(block, block, rs_send.at[4, h, i], rs_recv.at[4, h, i], who).start()
 

time: 77.6 us -> 77.1 us (level)
  no operation moved by 1% of the time
where the time goes in v5:
time: 77.1 us; the launch traced here: 77 us
  Pallas kernels  76.4 us (99%)
    pallas_call x1, Pallas kernels, shards(): pl.pallas_call(kernel, out_shape=[vmem((TOK, FEAT), BF16), vmem((RANK, FE...  72.5 us
    pallas_call x1, Pallas kernels, shards(): pl.pallas_call(finish, out_shape=[jax.ShapeDtypeStruct((TOK, FEAT), BF16)...  3.88 us

profile of v5, /device:TPU:1, one launch (start us, length us, event | category | flops | bytes accessed | tf_op | source)
XLA Modules:
  0.0 77.0 jit_solution(1207631189161549296)
XLA Ops:
  0.6 72.5 %gather_and_compress.1 = (bf16[1024,512]{1,0:T(8,128)(2,1)S(1)}, f32[32,512]{1,0:T(8,128)S(1)}, f32[192,8,128]{2,1,0:T(8,128)S(1)}, f32[12,512,512]{2,1,0:T(8,12...) custom-call(bf16[1024,512]{1,0:T(8,128)(2,1)} %acts_hbm.1, bf16[64,6144]{1,0:T(8,128)(2,1)} %grad_hbm.1, ...), custom_call_target="tpu_custom_call" | custom-call | flops 12884901888 | bytes 25165824 | tf_op jit(solution)/shard_map/gather_and_compress/pallas_call | solution.py:489
  73.1 3.9 %finish.1 = (bf16[1024,512]{1,0:T(8,128)(2,1)}, f32[32,512]{1,0:T(8,128)}, f32[32,6144]{1,0:T(8,128)}, bf16[512,6144]{1,0:T(8,128)(2,1)}) custom-call(bf16[1024,512]{1,0:T(8,128)(2,1)S(1)} %get-tuple-element.14.gin, f32[32,512]{1,0:T(8,128)S(1)} %get-tuple-element.15.p_t, f32[192,8,128]{2,1,0:T(8,128)S(1)} %get-tuple-element.16.q_all, ...), custom_call_target="tpu_custom_call" | custom-call | tf_op jit(solution)/shard_map/finish/pallas_call | solution.py:562
